TPU v7x, 256 devices: a whole 4x4x8 slice. The times are simulated.
256 devices in a mesh: replica: 16 (over z_hi, y, core), tp: 16 (over z_lo, x).
Axes of the slice: x: 4, y: 4, z: 8 (z_hi: 2, z_lo: 4; z = z_hi * 4 + z_lo), core: 2. Of those that a mesh axis runs over, the one named last changes fastest.
Arguments:
- weight_delta: bfloat16 [2048, 5120], P('tp', 'replica'), may hold values from -4 to 4
- rollout_copy: bfloat16 [16, 2048, 5120], P('replica', 'tp'), may hold values from -1.5 to 1.5
- cached_inputs: bfloat16 [32768, 5120], P('replica'), may hold values from -0.078125 to 0.078125
Outputs:
- renewed_weights: bfloat16 [16, 2048, 5120], P('replica', 'tp')
- keys_values: bfloat16 [32768, 2048], P('replica', 'tp')
All inputs are finite; a program needn't handle non-finite values.
Results may differ from a plain program's by a relative error of at most 0.0056.
Values may be sent and summed in bfloat16 or wider, within the bound.
No kernel may reach another device: no remote copies, remote signals or barrier semaphores. Data moves between devices by JAX's collectives and lax.ppermute only.
A program may use at most 64 MiB of HBM per device.

v0:
```python
import jax
import jax.numpy as jnp
from jax import lax
from jax.sharding import PartitionSpec as P

TILE = 128


EPSILON = 1e-06


def column_table(column_ids, tile_count):
    tile_of = column_ids // TILE
    return (tile_of[:, None] == lax.iota(jnp.int32, tile_count)[None, :]).astype(jnp.float32)


def expand_scale(tile_scale, column_ids):
    table = column_table(column_ids, tile_scale.shape[1])
    col_scale = jnp.dot(tile_scale, table.T, precision=lax.Precision.HIGHEST)
    return jnp.repeat(col_scale, TILE, axis=0)


def project_rows(token_rows, weights):
    return lax.dot_general(
        token_rows, weights, (((1,), (1,)), ((), ())), preferred_element_type=jnp.float32
    )


def on_device(weight_delta, rollout_copy, cached_inputs):
    row_count, piece_width = weight_delta.shape
    full_width = rollout_copy.shape[2]
    tile_count = full_width // TILE
    held_copy = rollout_copy[0]
    column_ids = lax.axis_index("replica") * piece_width + lax.iota(jnp.int32, piece_width)
    table = column_table(column_ids, tile_count)
    magnitude = jnp.abs(weight_delta.astype(jnp.float32)).reshape(
        row_count // TILE, TILE, piece_width
    )
    row_peak = jnp.max(magnitude, axis=1)
    partial_max = jnp.max(jnp.where(table[None, :, :] > 0.0, row_peak[:, :, None], 0.0), axis=1)
    tile_scale = lax.pmax(partial_max, "replica") + EPSILON
    piece_scale = expand_scale(tile_scale, column_ids)
    payload = (weight_delta.astype(jnp.float32) / piece_scale).astype(jnp.bfloat16)
    block_piece = lax.all_gather(payload, "replica", axis=1, tiled=True)
    block_width = block_piece.shape[1]
    block_ids = lax.iota(jnp.int32, block_width)
    block_scale = expand_scale(tile_scale, block_ids)
    restored_block = block_piece.astype(jnp.float32) * block_scale
    fresh_block = (held_copy.astype(jnp.float32) + restored_block).astype(jnp.bfloat16)
    running = project_rows(cached_inputs, fresh_block)
    return (fresh_block[None], running.astype(jnp.bfloat16))


def solution(mesh):
    placed = (P("tp", "replica"), P("replica", "tp", None), P("replica", None))
    return jax.shard_map(
        on_device,
        mesh=mesh,
        in_specs=placed,
        out_specs=(P("replica", "tp", None), P("replica", "tp")),
        check_vma=False,
    )
```

profile of v0, /device:TPU:1, one launch (start us, length us, event | category | flops | bytes accessed | tf_op | source)
XLA Modules:
  0.0 143.4 jit_solution(9950730213707313879)
XLA Ops:
  7.2 0.0 all-gather.2.cloned.1.call-start
  7.2 1.0 fusion.4
  8.2 0.1 select_reduce_fusion
  8.4 45.6 %pmax.7 = f32[1,40]{1,0:T(1,128)S(1)} all-reduce(f32[1,40]{1,0:T(1,128)S(1)} %bitcast.21), channel_id=1, replica_groups=mesh['replica'=16,'tp'=16] {'replica'}, use_global_device_ids=true, to_apply=%region_2.3 | all-reduce | flops 40 | bytes 320 | tf_op jit(solution)/shard_map/pmax | solution.py:41
  54.0 0.3 convolution_reduce_fusion
  54.3 1.6 %fusion.5 = bf16[128,320]{0,1:T(8,128)(2,1)} fusion(bf16[128,320]{0,1:T(8,128)(2,1)} %param.3, f32[320]{0:T(512)S(1)} %convolution_reduce_fusion), kind=kLoop, calls=%fused_computation.11 | loop fusion | flops 122880 | bytes 165120 | tf_op jit(solution)/shard_map/convert_element_type | solution.py:43
  55.9 0.0 all-gather.2.cloned.1.call-update
  55.9 1.8 %copy.10 = bf16[1,128,5120]{1,2,0:T(8,128)(2,1)S(1)} copy(bf16[1,128,5120]{2,1,0:T(8,128)(2,1)} %param.4) | data formatting | bytes 2621440 | tf_op args[1]
  57.7 0.4 fusion.2
  58.1 58.1 %all-gather.2.cloned.1.call-done = bf16[128,5120]{0,1:T(8,128)(2,1)} async-done(((bf16[128,320]{0,1:T(8,128)(2,1)}), bf16[128,5120]{0,1:T(8,128)(2,1)}) %all-gather.2.cloned.1.call-update) | async-done | bytes 1310736 | tf_op jit(solution)/shard_map/all_gather | solution.py:44
  116.2 0.0 copy-start
  116.2 4.2 %fusion.18 = bf16[1,128,5120]{1,2,0:T(8,128)(2,1)} fusion(f32[5120]{0:T(1024)S(1)} %bitcast.19, bf16[128,5120]{0,1:T(8,128)(2,1)} %all-gather.2.cloned.1.call-done, bf16[1,128,5120]{1,2,0:T(8,128)(2,1)S(1)} %copy.10), kind=kLoop, calls=%fused_computation.38 | loop fusion | flops 3276800 | bytes 3952640 | tf_op jit(solution)/shard_map/broadcast_in_dim | solution.py:51
  120.4 2.4 %copy.11 = bf16[1,128,5120]{2,1,0:T(8,128)(2,1)} copy(bf16[1,128,5120]{1,2,0:T(8,128)(2,1)} %fusion.18) | data formatting | bytes 2621440
  122.8 0.0 copy-done
  122.8 12.7 %fusion.1 = bf16[2048,128]{0,1:T(8,128)(2,1)S(1)} fusion(bf16[2048,5120]{1,0:T(8,128)(2,1)} %param.5, bf16[128,5120]{0,1:T(8,128)(2,1)S(1)} %copy-done, bf16[1,128,5120]{1,2,0:T(8,128)(2,1)S(1)} %copy.10, f32[5120]{0:T(1024)S(1)} %bitcast.20), kind=kOutput, calls=%fused_computation.3 | convolution fusion | flops 2687893504 | bytes 24137728 | tf_op jit(solution)/shard_map/dot_general | solution.py:24
  135.6 1.0 copy.12
  (2 shorter events, 0.0 us)
Async XLA Ops:
  7.2 109.0 %all-gather.2.cloned.1.call-start = ((), (), s32[]{:S(2)}) async-start(), calls=%async_computation | async-start | bytes 1392640 | tf_op jit(solution)/shard_map/all_gather | solution.py:44
  116.2 6.6 %copy-start = (bf16[128,5120]{0,1:T(8,128)(2,1)S(1)}, bf16[128,5120]{0,1:T(8,128)(2,1)}, u32[]{:S(2)}) copy-start(bf16[128,5120]{0,1:T(8,128)(2,1)} %all-gather.2.cloned.1.call-done) | copy-start | bytes 3932164
Sparse Core Ops, SparseCore 0:
  56.1 60.1 all-gather.1
where the time goes:
time: 144 us; the launch traced here: 143 us
  waiting for transfers between devices  58.1 us (40%)
  blocking collectives  45.6 us (32%)
  between operations  14.1 us (10%)
  matrix products  13.4 us (9%)
  other arithmetic  6.97 us (5%)
  local copies, waits for them, and re-layouts  5.19 us (4%)
    all_gather x1, waiting for transfers between devices, on_device(): block_piece = lax.all_gather(payload, 'replica', axis=1, tiled=True)  58.1 us
    pmax x1, blocking collectives, on_device(): tile_scale = lax.pmax(partial_max, 'replica') + EPSILON  45.6 us
    dot_general x1, matrix products, project_rows(): lax.dot_general(token_rows, weights, (((1,), (1,)), ((), ())), preferred_...  12.7 us
    unnamed x5, local copies, waits for them, and re-layouts  5.19 us
    broadcast_in_dim x1, other arithmetic, on_device(): return (fresh_block[None], running.astype(jnp.bfloat16))  4.2 us
  transfers between devices with their start and end apart: 1, of which 1 were waited for; matrix products, arithmetic and copies ran while one was open for 1% of the time, Pallas kernels for 0%

commit v1 on v0

v1 whole, which is shorter than its diff:
```python
import functools

import jax
import jax.numpy as jnp
from jax import lax
from jax.experimental import pallas as pl
from jax.experimental.pallas import tpu as pltpu
from jax.sharding import PartitionSpec as P

TILE = 128
EPSILON = 1e-06
STEPS = (2, 1, 3)
TOKEN_BLOCK = 512

NT = (((1,), (1,)), ((), ()))


def moved(dz=0, dy=0, dc=0):
    pairs = []
    for source in range(16):
        z, y, core = source >> 3, (source >> 1) & 3, source & 1
        pairs.append((source, ((z + dz) % 2) * 8 + ((y + dy) % 4) * 2 + (core + dc) % 2))
    return pairs


def send(value, **offset):
    return lax.ppermute(value, "replica", moved(**offset))


def whereabouts():
    replica = lax.axis_index("replica")
    return replica >> 3, (replica >> 1) & 3, replica & 1


def renew_half(place, pieces, swapped, held, delta, weights, half):
    piece_rows = pieces[0].shape[0]
    half_width = delta.shape[0]
    _, y, core = place
    for index, step in enumerate((0,) + STEPS):
        chip = lax.rem(y + 4 - step, 4)
        base = chip * (2 * piece_rows)
        mine = pl.multiple_of(base + core * piece_rows, 64)
        other = pl.multiple_of(base + (1 - core) * piece_rows, 64)
        delta[pl.ds(mine, piece_rows), :] = pieces[index][...]
        delta[pl.ds(other, piece_rows), :] = swapped[index * piece_rows : (index + 1) * piece_rows, :]
    row = lax.broadcasted_iota(jnp.int32, (TILE, TILE), 0)
    col = lax.broadcasted_iota(jnp.int32, (TILE, TILE), 1)
    identity = (row == col).astype(jnp.bfloat16)
    start = half * half_width
    for t in range(half_width // TILE):
        tile = delta[t * TILE : (t + 1) * TILE, :].astype(jnp.float32)
        scale = jnp.max(jnp.abs(tile), axis=(0, 1), keepdims=True) + EPSILON
        normalized = (tile / scale).astype(jnp.bfloat16)
        turned = lax.dot_general(identity, normalized, NT, preferred_element_type=jnp.float32)
        columns = pl.ds(pl.multiple_of(start + t * TILE, TILE), TILE)
        fresh = held[:, columns].astype(jnp.float32) + turned * scale
        weights[:, t * TILE : (t + 1) * TILE] = fresh.astype(jnp.bfloat16)


def first_kernel(p0, p1, p2, p3, swapped, held, tokens, weights, partial, delta):
    place = whereabouts()
    half = place[0]
    renew_half(place, (p0, p1, p2, p3), swapped, held, delta, weights, half)
    width = weights.shape[1]
    columns = pl.ds(pl.multiple_of(half * width, TILE), width)

    @pl.loop(0, tokens.shape[0] // TOKEN_BLOCK)
    def _(block):
        rows = pl.ds(pl.multiple_of(block * TOKEN_BLOCK, TOKEN_BLOCK), TOKEN_BLOCK)
        partial[rows, :] = lax.dot_general(
            tokens[rows, columns], weights[...], NT, preferred_element_type=jnp.float32
        )


def second_kernel(
    p0, p1, p2, p3, swapped, held, tokens, near_weights, partial,
    renewed, result, delta, far_weights, near_sem, far_sem,
):
    place = whereabouts()
    near, far = place[0], 1 - place[0]
    width = far_weights.shape[1]
    near_columns = pl.ds(pl.multiple_of(near * width, TILE), width)
    far_columns = pl.ds(pl.multiple_of(far * width, TILE), width)
    near_copy = pltpu.make_async_copy(near_weights, renewed.at[:, near_columns], near_sem)
    near_copy.start()
    renew_half(place, (p0, p1, p2, p3), swapped, held, delta, far_weights, far)
    far_copy = pltpu.make_async_copy(far_weights, renewed.at[:, far_columns], far_sem)
    far_copy.start()

    @pl.loop(0, tokens.shape[0] // TOKEN_BLOCK)
    def _(block):
        rows = pl.ds(pl.multiple_of(block * TOKEN_BLOCK, TOKEN_BLOCK), TOKEN_BLOCK)
        result[rows, :] = (
            partial[rows, :]
            + lax.dot_general(
                tokens[rows, far_columns], far_weights[...], NT, preferred_element_type=jnp.float32
            )
        ).astype(jnp.bfloat16)

    near_copy.wait()
    far_copy.wait()


VMEM = pl.BlockSpec(memory_space=pltpu.VMEM)
ANY = pl.BlockSpec(memory_space=pl.ANY)


def on_device(weight_delta, rollout_copy, cached_inputs):
    row_count, piece_width = weight_delta.shape
    full_width = rollout_copy.shape[2]
    token_count = cached_inputs.shape[0]
    half_width = full_width // 2
    piece = weight_delta.T
    tokens = pltpu.with_memory_space_constraint(cached_inputs, pltpu.VMEM)
    held = pltpu.with_memory_space_constraint(rollout_copy[0], pltpu.VMEM)

    far_piece = send(piece, dz=1)
    near = [piece] + [send(piece, dy=step) for step in STEPS]
    near_swapped = send(jnp.concatenate(near), dc=1)
    far = [far_piece] + [send(far_piece, dy=step) for step in STEPS]
    far_swapped = send(jnp.concatenate(far), dc=1)

    flops = 2 * token_count * row_count * half_width
    near_weights, partial = pl.pallas_call(
        first_kernel,
        out_shape=(
            pltpu.VMEM((row_count, half_width), jnp.bfloat16),
            pltpu.VMEM((token_count, row_count), jnp.float32),
        ),
        in_specs=[VMEM] * 7,
        out_specs=(VMEM, VMEM),
        scratch_shapes=[pltpu.VMEM((half_width, row_count), jnp.bfloat16)],
        compiler_params=pltpu.CompilerParams(vmem_limit_bytes=16 * 2**20),
        cost_estimate=pl.CostEstimate(flops=flops, bytes_accessed=8 * 2**20, transcendentals=0),
    )(*near, near_swapped, held, tokens)
    renewed, result = pl.pallas_call(
        second_kernel,
        out_shape=(
            jax.ShapeDtypeStruct((row_count, full_width), jnp.bfloat16),
            jax.ShapeDtypeStruct((token_count, row_count), jnp.bfloat16),
        ),
        in_specs=[VMEM] * 9,
        out_specs=(ANY, VMEM),
        scratch_shapes=[
            pltpu.VMEM((half_width, row_count), jnp.bfloat16),
            pltpu.VMEM((row_count, half_width), jnp.bfloat16),
            pltpu.SemaphoreType.DMA,
            pltpu.SemaphoreType.DMA,
        ],
        compiler_params=pltpu.CompilerParams(vmem_limit_bytes=16 * 2**20),
        cost_estimate=pl.CostEstimate(flops=flops, bytes_accessed=8 * 2**20, transcendentals=0),
    )(*far, far_swapped, held, tokens, near_weights, partial)
    return (renewed[None], result)


def solution(mesh):
    placed = (P("tp", "replica"), P("replica", "tp", None), P("replica", None))
    return jax.shard_map(
        on_device,
        mesh=mesh,
        in_specs=placed,
        out_specs=(P("replica", "tp", None), P("replica", "tp")),
        check_vma=False,
    )
```

time: 144 us -> 42.9 us (0.30)
  waiting for transfers between devices: 58.1 us -> 0.58 us
  blocking collectives: 45.6 us -> 0 us
  starting transfers between devices: 0.04 us -> 20.7 us
  between operations: 14.1 us -> 0.68 us
  matrix products: 13.4 us -> 0 us
  Pallas kernels: 0 us -> 9.1 us
  other arithmetic: 6.97 us -> 0.93 us
  local copies, waits for them, and re-layouts: 5.19 us -> 10.7 us
    all_gather x1 -> x0, waiting for transfers between devices: 58.1 us -> none  [on_device(): block_piece = lax.all_gather(payload, 'replica', axis=1, tiled=True)]
    pmax x1 -> x0, blocking collectives: 45.6 us -> none  [on_device(): tile_scale = lax.pmax(partial_max, 'replica') + EPSILON]
    ppermute x0 -> x9, starting transfers between devices: none -> 20.7 us  [send(): return lax.ppermute(value, 'replica', moved(**offset))]
    dot_general x3 -> x0, matrix products: 13.4 us -> none  [the longest x1 12.7 us: project_rows(): lax.dot_general(token_rows, weights, (((1,), (1,)), ((), ())), preferred_...]
    pallas_call x0 -> x2, Pallas kernels: none -> 9.1 us  [the longest x1 5 us: on_device(): pl.pallas_call(second_kernel, out_shape=(jax.ShapeDtypeStruct((row_count,...]
    unnamed x5 -> x8, local copies, waits for them, and re-layouts: 5.19 us -> 10.7 us
    broadcast_in_dim x1 -> x0, other arithmetic: 4.2 us -> none  [on_device(): return (fresh_block[None], running.astype(jnp.bfloat16))]
    convert_element_type x1 -> x0, other arithmetic: 1.64 us -> none  [on_device(): (weight_delta.astype(jnp.float32) / piece_scale).astype(jnp.bfloat16)]
  transfers between devices with their start and end apart: 1 -> 9, of which waited for: 1 -> 1; matrix products, arithmetic and copies ran while one was open for 1% -> 2% of each run, Pallas kernels for 0% -> 10%
where the time goes in v1:
time: 42.9 us; the launch traced here: 42.7 us
  starting transfers between devices  20.7 us (48%)
  local copies, waits for them, and re-layouts  10.7 us (25%)
  Pallas kernels  9.1 us (21%)
  other arithmetic  0.93 us (2%)
  between operations  0.68 us (2%)
  waiting for transfers between devices  0.58 us (1%)
    ppermute x9, starting transfers between devices, send(): return lax.ppermute(value, 'replica', moved(**offset))  20.7 us
    unnamed x8, local copies, waits for them, and re-layouts  10.7 us
    pallas_call x1, Pallas kernels, on_device(): pl.pallas_call(second_kernel, out_shape=(jax.ShapeDtypeStruct((row_count,...  5 us
    pallas_call x1, Pallas kernels, on_device(): pl.pallas_call(first_kernel, out_shape=(pltpu.VMEM((row_count, half_width...  4.1 us
    concatenate x1, other arithmetic, on_device(): near_swapped = send(jnp.concatenate(near), dc=1)  0.91 us
  transfers between devices with their start and end apart: 9, of which 1 were waited for; matrix products, arithmetic and copies ran while one was open for 2% of the time, Pallas kernels for 10%

profile of v1, /device:TPU:1, one launch (start us, length us, event | category | flops | bytes accessed | tf_op | source)
XLA Modules:
  0.0 42.7 jit_solution(17762292427081593656)
XLA Ops:
  0.6 0.0 copy-start.2
  0.6 7.8 %collective-permute-start = (bf16[320,128]{1,0:T(8,128)(2,1)}, bf16[320,128]{1,0:T(8,128)(2,1)S(1)}, u32[]{:S(2)}, u32[]{:S(2)}) collective-permute-start(bf16[320,128]{1,0:T(8,128)(2,1)} %bitcast.5), channel_id=1, source_target_pairs={{0,128},{16,144},{32,160},{48,176},{64,192},{80,208},{96,224},{112... | collective-permute-start | bytes 245768 | tf_op jit(solution)/shard_map/ppermute | solution.py:27
  8.5 2.7 %collective-permute-start.7 = (bf16[320,128]{1,0:T(8,128)(2,1)}, bf16[320,128]{1,0:T(8,128)(2,1)S(1)}, u32[]{:S(2)}, u32[]{:S(2)}) collective-permute-start(bf16[320,128]{1,0:T(8,128)(2,1)} %bitcast.6), channel_id=1, source_target_pairs={{0,96},{16,112},{32,0},{48,16},{64,32},{80,48},{96,64},{112,80},{1... | collective-permute-start | bytes 245768 | tf_op jit(solution)/shard_map/ppermute | solution.py:27
  11.2 0.0 collective-permute-start.6
  11.2 1.6 %collective-permute-start.5 = (bf16[320,128]{1,0:T(8,128)(2,1)}, bf16[320,128]{1,0:T(8,128)(2,1)S(1)}, u32[]{:S(2)}, u32[]{:S(2)}) collective-permute-start(bf16[320,128]{1,0:T(8,128)(2,1)} %bitcast.8), channel_id=1, source_target_pairs={{0,64},{16,80},{32,96},{48,112},{64,0},{80,16},{96,32},{112,48},{1... | collective-permute-start | bytes 245768 | tf_op jit(solution)/shard_map/ppermute | solution.py:27
  12.8 0.0 collective-permute-done.p0
  12.8 1.0 %collective-permute-start.3 = (bf16[320,128]{1,0:T(8,128)(2,1)S(1)}, bf16[320,128]{1,0:T(8,128)(2,1)S(1)}, u32[]{:S(2)}, u32[]{:S(2)}) collective-permute-start(bf16[320,128]{1,0:T(8,128)(2,1)S(1)} %collective-permute-done.p0), channel_id=1, source_target_pairs={{0,96},{16,112},{32,0},{48,16},{64,32},{80,48},{96,64},{112,80},{1... | collective-permute-start | bytes 245768 | tf_op jit(solution)/shard_map/ppermute | solution.py:27
  13.9 0.6 %collective-permute-start.2 = (bf16[320,128]{1,0:T(8,128)(2,1)S(1)}, bf16[320,128]{1,0:T(8,128)(2,1)S(1)}, u32[]{:S(2)}, u32[]{:S(2)}) collective-permute-start(bf16[320,128]{1,0:T(8,128)(2,1)S(1)} %collective-permute-done.p0), channel_id=1, source_target_pairs={{0,32},{16,48},{32,64},{48,80},{64,96},{80,112},{96,0},{112,16},{1... | collective-permute-start | bytes 245768 | tf_op jit(solution)/shard_map/ppermute | solution.py:27
  14.5 0.0 collective-permute-done.7.p3
  14.5 1.8 %collective-permute-start.1 = (bf16[320,128]{1,0:T(8,128)(2,1)S(1)}, bf16[320,128]{1,0:T(8,128)(2,1)S(1)}, u32[]{:S(2)}, u32[]{:S(2)}) collective-permute-start(bf16[320,128]{1,0:T(8,128)(2,1)S(1)} %collective-permute-done.p0), channel_id=1, source_target_pairs={{0,64},{16,80},{32,96},{48,112},{64,0},{80,16},{96,32},{112,48},{1... | collective-permute-start | bytes 245768 | tf_op jit(solution)/shard_map/ppermute | solution.py:27
  16.3 0.5 %collective-permute-done.6.p2 = bf16[320,128]{1,0:T(8,128)(2,1)S(1)} collective-permute-done((bf16[320,128]{1,0:T(8,128)(2,1)}, bf16[320,128]{1,0:T(8,128)(2,1)S(1)}, u32[]{:S(2)}, u32[]{:S(2)}) %collective-permute-start.6) | collective-permute-done | bytes 81952 | tf_op jit(solution)/shard_map/ppermute | solution.py:27
  16.8 0.0 collective-permute-done.5.p1
  16.8 0.9 %pad_maximum_fusion.1 = bf16[1280,128]{1,0:T(8,128)(2,1)S(1)} fusion(bf16[320,128]{1,0:T(8,128)(2,1)S(1)} %collective-permute-done.7.p3, bf16[320,128]{1,0:T(8,128)(2,1)S(1)} %collective-permute-done.6.p2, bf16[320,128]{1,0:T(8,128)(2,1)S(1)} %collective-permute-done.5.p1, bf16[320,128]{1,0:T(8,128)(2,1)} %bitcast.9), kind=kLoop, calls=%fused_computation.1 | loop fusion | flops 1310720 | bytes 655360 | tf_op jit(solution)/shard_map/concatenate | solution.py:119
  17.7 3.9 %collective-permute-start.8 = (bf16[1280,128]{1,0:T(8,128)(2,1)S(1)}, bf16[1280,128]{1,0:T(8,128)(2,1)S(1)}, u32[]{:S(2)}, u32[]{:S(2)}) collective-permute-start(bf16[1280,128]{1,0:T(8,128)(2,1)S(1)} %pad_maximum_fusion.1), channel_id=1, source_target_pairs={{0,16},{16,0},{32,48},{48,32},{64,80},{80,64},{96,112},{112,96},{1... | collective-permute-start | bytes 983048 | tf_op jit(solution)/shard_map/ppermute | solution.py:27
  21.6 0.0 collective-permute-done.3.p3
  21.6 0.0 collective-permute-done.2.p2
  21.6 0.0 collective-permute-done.1.p1
  21.6 1.2 %collective-permute-start.4 = (bf16[1280,128]{1,0:T(8,128)(2,1)S(1)}, bf16[1280,128]{1,0:T(8,128)(2,1)S(1)}, u32[]{:S(2)}, u32[]{:S(2)}) collective-permute-start(bf16[1280,128]{1,0:T(8,128)(2,1)S(1)} %pad_maximum_fusion), channel_id=1, source_target_pairs={{0,16},{16,0},{32,48},{48,32},{64,80},{80,64},{96,112},{112,96},{1... | collective-permute-start | bytes 983048 | tf_op jit(solution)/shard_map/ppermute | solution.py:27
  22.9 0.0 collective-permute-done.8.swapped
  22.9 0.0 copy-done.2
  22.9 0.0 copy-start
  22.9 7.0 %copy-done = bf16[2048,5120]{1,0:T(8,128)(2,1)S(1)} copy-done((bf16[2048,5120]{1,0:T(8,128)(2,1)S(1)}, bf16[2048,5120]{1,0:T(8,128)(2,1)}, u32[]{:S(2)}) %copy-start) | copy-done | bytes 20971544
  29.8 0.0 copy-start.3
  29.8 0.9 %copy-done.3 = bf16[128,320]{0,1:T(8,128)(2,1)S(1)} copy-done((bf16[128,320]{0,1:T(8,128)(2,1)S(1)}, bf16[128,320]{0,1:T(8,128)(2,1)}, u32[]{:S(2)}) %copy-start.3) | copy-done | bytes 81944
  30.7 0.0 copy-start.1
  30.7 4.1 %shard_map.50 = (bf16[128,2560]{1,0:T(8,128)(2,1)S(1)}, f32[2048,128]{1,0:T(8,128)S(1)}) custom-call(bf16[320,128]{1,0:T(8,128)(2,1)S(1)} %bitcast.10, bf16[320,128]{1,0:T(8,128)(2,1)S(1)} %collective-permute-done.5.p1, bf16[320,128]{1,0:T(8,128)(2,1)S(1)} %collective-permute-done.6.p2, bf16[320,128]{1,0:T(8,128)(2,1)S(1)} %collective-permute-done.7.p3, ...), custom_call_target="tpu_custom_call" | custom-call | flops 1342177280 | bytes 8388608 | tf_op jit(solution)/shard_map/pallas_call | solution.py:124
  34.8 0.0 collective-permute-done.4.swapped
  34.8 2.8 %copy-done.1 = bf16[2048,5120]{1,0:T(8,128)(2,1)S(1)} copy-done((bf16[2048,5120]{1,0:T(8,128)(2,1)S(1)}, bf16[2048,5120]{1,0:T(8,128)(2,1)}, u32[]{:S(2)}) %copy-start.1) | copy-done | bytes 20971544
  37.7 5.0 %shard_map.51 = (bf16[128,5120]{1,0:T(8,128)(2,1)}, bf16[2048,128]{1,0:T(8,128)(2,1)}) custom-call(bf16[320,128]{1,0:T(8,128)(2,1)S(1)} %collective-permute-done.p0, bf16[320,128]{1,0:T(8,128)(2,1)S(1)} %collective-permute-done.1.p1, bf16[320,128]{1,0:T(8,128)(2,1)S(1)} %collective-permute-done.2.p2, bf16[320,128]{1,0:T(8,128)(2,1)S(1)} %collective-permute-done.3.p3, ...), custom_call_target="tpu_custom_call" | custom-call | flops 1342177280 | bytes 8388608 | tf_op jit(solution)/shard_map/pallas_call | solution.py:136
  (1 shorter events, 0.0 us)
Async XLA Ops:
  0.6 22.2 %copy-start.2 = (bf16[1,128,5120]{2,1,0:T(8,128)(2,1)S(1)}, bf16[1,128,5120]{2,1,0:T(8,128)(2,1)}, u32[]{:S(2)}) copy-start(bf16[1,128,5120]{2,1,0:T(8,128)(2,1)} %param.4) | copy-start | bytes 3932164
  0.6 12.2 %collective-permute-start = (bf16[320,128]{1,0:T(8,128)(2,1)}, bf16[320,128]{1,0:T(8,128)(2,1)S(1)}, u32[]{:S(2)}, u32[]{:S(2)}) collective-permute-start(bf16[320,128]{1,0:T(8,128)(2,1)} %bitcast.5), channel_id=1, source_target_pairs={{0,128},{16,144},{32,160},{48,176},{64,192},{80,208},{96,224},{112... | collective-permute-start | bytes 245768 | tf_op jit(solution)/shard_map/ppermute | solution.py:27
  8.5 6.0 %collective-permute-start.7 = (bf16[320,128]{1,0:T(8,128)(2,1)}, bf16[320,128]{1,0:T(8,128)(2,1)S(1)}, u32[]{:S(2)}, u32[]{:S(2)}) collective-permute-start(bf16[320,128]{1,0:T(8,128)(2,1)} %bitcast.6), channel_id=1, source_target_pairs={{0,96},{16,112},{32,0},{48,16},{64,32},{80,48},{96,64},{112,80},{1... | collective-permute-start | bytes 245768 | tf_op jit(solution)/shard_map/ppermute | solution.py:27
  11.2 5.6 %collective-permute-start.6 = (bf16[320,128]{1,0:T(8,128)(2,1)}, bf16[320,128]{1,0:T(8,128)(2,1)S(1)}, u32[]{:S(2)}, u32[]{:S(2)}) collective-permute-start(bf16[320,128]{1,0:T(8,128)(2,1)} %bitcast.7), channel_id=1, source_target_pairs={{0,32},{16,48},{32,64},{48,80},{64,96},{80,112},{96,0},{112,16},{1... | collective-permute-start | bytes 245768 | tf_op jit(solution)/shard_map/ppermute | solution.py:27
  11.2 5.6 %collective-permute-start.5 = (bf16[320,128]{1,0:T(8,128)(2,1)}, bf16[320,128]{1,0:T(8,128)(2,1)S(1)}, u32[]{:S(2)}, u32[]{:S(2)}) collective-permute-start(bf16[320,128]{1,0:T(8,128)(2,1)} %bitcast.8), channel_id=1, source_target_pairs={{0,64},{16,80},{32,96},{48,112},{64,0},{80,16},{96,32},{112,48},{1... | collective-permute-start | bytes 245768 | tf_op jit(solution)/shard_map/ppermute | solution.py:27
  12.8 8.7 %collective-permute-start.3 = (bf16[320,128]{1,0:T(8,128)(2,1)S(1)}, bf16[320,128]{1,0:T(8,128)(2,1)S(1)}, u32[]{:S(2)}, u32[]{:S(2)}) collective-permute-start(bf16[320,128]{1,0:T(8,128)(2,1)S(1)} %collective-permute-done.p0), channel_id=1, source_target_pairs={{0,96},{16,112},{32,0},{48,16},{64,32},{80,48},{96,64},{112,80},{1... | collective-permute-start | bytes 245768 | tf_op jit(solution)/shard_map/ppermute | solution.py:27
  13.9 7.7 %collective-permute-start.2 = (bf16[320,128]{1,0:T(8,128)(2,1)S(1)}, bf16[320,128]{1,0:T(8,128)(2,1)S(1)}, u32[]{:S(2)}, u32[]{:S(2)}) collective-permute-start(bf16[320,128]{1,0:T(8,128)(2,1)S(1)} %collective-permute-done.p0), channel_id=1, source_target_pairs={{0,32},{16,48},{32,64},{48,80},{64,96},{80,112},{96,0},{112,16},{1... | collective-permute-start | bytes 245768 | tf_op jit(solution)/shard_map/ppermute | solution.py:27
  14.5 7.1 %collective-permute-start.1 = (bf16[320,128]{1,0:T(8,128)(2,1)S(1)}, bf16[320,128]{1,0:T(8,128)(2,1)S(1)}, u32[]{:S(2)}, u32[]{:S(2)}) collective-permute-start(bf16[320,128]{1,0:T(8,128)(2,1)S(1)} %collective-permute-done.p0), channel_id=1, source_target_pairs={{0,64},{16,80},{32,96},{48,112},{64,0},{80,16},{96,32},{112,48},{1... | collective-permute-start | bytes 245768 | tf_op jit(solution)/shard_map/ppermute | solution.py:27
  17.7 5.1 %collective-permute-start.8 = (bf16[1280,128]{1,0:T(8,128)(2,1)S(1)}, bf16[1280,128]{1,0:T(8,128)(2,1)S(1)}, u32[]{:S(2)}, u32[]{:S(2)}) collective-permute-start(bf16[1280,128]{1,0:T(8,128)(2,1)S(1)} %pad_maximum_fusion.1), channel_id=1, source_target_pairs={{0,16},{16,0},{32,48},{48,32},{64,80},{80,64},{96,112},{112,96},{1... | collective-permute-start | bytes 983048 | tf_op jit(solution)/shard_map/ppermute | solution.py:27
  21.6 13.2 %collective-permute-start.4 = (bf16[1280,128]{1,0:T(8,128)(2,1)S(1)}, bf16[1280,128]{1,0:T(8,128)(2,1)S(1)}, u32[]{:S(2)}, u32[]{:S(2)}) collective-permute-start(bf16[1280,128]{1,0:T(8,128)(2,1)S(1)} %pad_maximum_fusion), channel_id=1, source_target_pairs={{0,16},{16,0},{32,48},{48,32},{64,80},{80,64},{96,112},{112,96},{1... | collective-permute-start | bytes 983048 | tf_op jit(solution)/shard_map/ppermute | solution.py:27
  22.9 7.0 %copy-start = (bf16[2048,5120]{1,0:T(8,128)(2,1)S(1)}, bf16[2048,5120]{1,0:T(8,128)(2,1)}, u32[]{:S(2)}) copy-start(bf16[2048,5120]{1,0:T(8,128)(2,1)} %tokens.3) | copy-start | bytes 62914564
  29.8 0.9 %copy-start.3 = (bf16[128,320]{0,1:T(8,128)(2,1)S(1)}, bf16[128,320]{0,1:T(8,128)(2,1)}, u32[]{:S(2)}) copy-start(bf16[128,320]{0,1:T(8,128)(2,1)} %param.3) | copy-start | bytes 245764
  30.7 7.0 %copy-start.1 = (bf16[2048,5120]{1,0:T(8,128)(2,1)S(1)}, bf16[2048,5120]{1,0:T(8,128)(2,1)}, u32[]{:S(2)}) copy-start(bf16[2048,5120]{1,0:T(8,128)(2,1)} %tokens.3) | copy-start | bytes 62914564

commit v2 on v1

--- a/solution.py
+++ b/solution.py
@@ -101,6 +101,12 @@
     far_copy.wait()
 
 
+def stage_kernel(piece, staged, sem):
+    copy = pltpu.make_async_copy(piece, staged, sem)
+    copy.start()
+    copy.wait()
+
+
 VMEM = pl.BlockSpec(memory_space=pltpu.VMEM)
 ANY = pl.BlockSpec(memory_space=pl.ANY)
 
@@ -115,7 +121,16 @@
     held = pltpu.with_memory_space_constraint(rollout_copy[0], pltpu.VMEM)
 
     far_piece = send(piece, dz=1)
-    near = [piece] + [send(piece, dy=step) for step in STEPS]
+    staged = pl.pallas_call(
+        stage_kernel,
+        out_shape=pltpu.VMEM(piece.shape, piece.dtype),
+        in_specs=[ANY],
+        out_specs=VMEM,
+        scratch_shapes=[pltpu.SemaphoreType.DMA],
+        compiler_params=pltpu.CompilerParams(vmem_limit_bytes=2**20),
+        cost_estimate=pl.CostEstimate(flops=10**10, bytes_accessed=24 * 2**20, transcendentals=0),
+    )(pltpu.with_memory_space_constraint(piece, pltpu.HBM))
+    near = [staged] + [send(staged, dy=step) for step in STEPS]
     near_swapped = send(jnp.concatenate(near), dc=1)
     far = [far_piece] + [send(far_piece, dy=step) for step in STEPS]
     far_swapped = send(jnp.concatenate(far), dc=1)

time: 42.9 us -> 33.1 us (0.77)
  local copies, waits for them, and re-layouts: 10.7 us -> 0.03 us
  starting transfers between devices: 20.7 us -> 21.6 us
  Pallas kernels: 9.1 us -> 10 us
  other arithmetic: 0.93 us -> 0.04 us
    unnamed x8 -> x12, local copies, waits for them, and re-layouts: 10.7 us -> 0.03 us
    pallas_call x0 -> x1, Pallas kernels: none -> 0.93 us  [on_device(): pl.pallas_call(stage_kernel, out_shape=pltpu.VMEM(piece.shape, piece.dtyp...]
    ppermute x9, starting transfers between devices: 20.7 us -> 21.6 us  [send(): return lax.ppermute(value, 'replica', moved(**offset))]
    concatenate x1, other arithmetic: 0.91 us -> 0.02 us  [on_device(): near_swapped = send(jnp.concatenate(near), dc=1)]
  transfers between devices with their start and end apart: 9 -> 9, of which waited for: 1 -> 2; matrix products, arithmetic and copies ran while one was open for 2% -> 0% of each run, Pallas kernels for 10% -> 15%
where the time goes in v2:
time: 33.1 us; the launch traced here: 33 us
  starting transfers between devices  21.6 us (65%)
  Pallas kernels  10 us (30%)
  between operations  0.76 us (2%)
  waiting for transfers between devices  0.5 us (2%)
    ppermute x9, starting transfers between devices, send(): return lax.ppermute(value, 'replica', moved(**offset))  21.6 us
    pallas_call x1, Pallas kernels, on_device(): pl.pallas_call(second_kernel, out_shape=(jax.ShapeDtypeStruct((row_count,...  5 us
    pallas_call x1, Pallas kernels, on_device(): pl.pallas_call(first_kernel, out_shape=(pltpu.VMEM((row_count, half_width...  4.11 us
    pallas_call x1, Pallas kernels, on_device(): pl.pallas_call(stage_kernel, out_shape=pltpu.VMEM(piece.shape, piece.dtyp...  0.93 us
  transfers between devices with their start and end apart: 9, of which 2 were waited for; matrix products, arithmetic and copies ran while one was open for 0% of the time, Pallas kernels for 15%

profile of v2, /device:TPU:1, one launch (start us, length us, event | category | flops | bytes accessed | tf_op | source)
XLA Modules:
  0.0 33.0 jit_solution(1383899436612918306)
XLA Ops:
  0.6 0.0 slice-start
  0.6 0.0 slice-start.1
  0.7 0.0 slice-start.2
  0.7 0.0 slice-start.3
  0.7 0.0 slice-start.4
  0.7 7.8 %collective-permute-start = (bf16[320,128]{1,0:T(8,128)(2,1)}, bf16[320,128]{1,0:T(8,128)(2,1)S(1)}, u32[]{:S(2)}, u32[]{:S(2)}) collective-permute-start(bf16[320,128]{1,0:T(8,128)(2,1)} %bitcast.8), channel_id=1, source_target_pairs={{0,128},{16,144},{32,160},{48,176},{64,192},{80,208},{96,224},{112... | collective-permute-start | bytes 245768 | tf_op jit(solution)/shard_map/ppermute | solution.py:27
  8.5 0.9 %shard_map.50.p0 = bf16[320,128]{1,0:T(8,128)(2,1)S(1)} custom-call(bf16[320,128]{1,0:T(8,128)(2,1)} %bitcast.9), custom_call_target="tpu_custom_call" | custom-call | flops 10000000000 | bytes 25165824 | tf_op jit(solution)/shard_map/pallas_call | solution.py:124
  9.4 0.0 copy-start
  9.5 2.8 %collective-permute-start.7 = (bf16[320,128]{1,0:T(8,128)(2,1)S(1)}, bf16[320,128]{1,0:T(8,128)(2,1)S(1)}, u32[]{:S(2)}, u32[]{:S(2)}) collective-permute-start(bf16[320,128]{1,0:T(8,128)(2,1)S(1)} %shard_map.50.p0), channel_id=1, source_target_pairs={{0,96},{16,112},{32,0},{48,16},{64,32},{80,48},{96,64},{112,80},{1... | collective-permute-start | bytes 245768 | tf_op jit(solution)/shard_map/ppermute | solution.py:27
  12.3 0.0 collective-permute-start.6
  12.3 1.6 %collective-permute-start.5 = (bf16[320,128]{1,0:T(8,128)(2,1)S(1)}, bf16[320,128]{1,0:T(8,128)(2,1)S(1)}, u32[]{:S(2)}, u32[]{:S(2)}) collective-permute-start(bf16[320,128]{1,0:T(8,128)(2,1)S(1)} %shard_map.50.p0), channel_id=1, source_target_pairs={{0,64},{16,80},{32,96},{48,112},{64,0},{80,16},{96,32},{112,48},{1... | collective-permute-start | bytes 245768 | tf_op jit(solution)/shard_map/ppermute | solution.py:27
  13.9 0.0 collective-permute-done.p0
  13.9 1.0 %collective-permute-start.3 = (bf16[320,128]{1,0:T(8,128)(2,1)S(1)}, bf16[320,128]{1,0:T(8,128)(2,1)S(1)}, u32[]{:S(2)}, u32[]{:S(2)}) collective-permute-start(bf16[320,128]{1,0:T(8,128)(2,1)S(1)} %collective-permute-done.p0), channel_id=1, source_target_pairs={{0,96},{16,112},{32,0},{48,16},{64,32},{80,48},{96,64},{112,80},{1... | collective-permute-start | bytes 245768 | tf_op jit(solution)/shard_map/ppermute | solution.py:27
  15.0 0.6 %collective-permute-start.2 = (bf16[320,128]{1,0:T(8,128)(2,1)S(1)}, bf16[320,128]{1,0:T(8,128)(2,1)S(1)}, u32[]{:S(2)}, u32[]{:S(2)}) collective-permute-start(bf16[320,128]{1,0:T(8,128)(2,1)S(1)} %collective-permute-done.p0), channel_id=1, source_target_pairs={{0,32},{16,48},{32,64},{48,80},{64,96},{80,112},{96,0},{112,16},{1... | collective-permute-start | bytes 245768 | tf_op jit(solution)/shard_map/ppermute | solution.py:27
  15.5 0.0 collective-permute-done.7.p3
  15.5 1.8 %collective-permute-start.1 = (bf16[320,128]{1,0:T(8,128)(2,1)S(1)}, bf16[320,128]{1,0:T(8,128)(2,1)S(1)}, u32[]{:S(2)}, u32[]{:S(2)}) collective-permute-start(bf16[320,128]{1,0:T(8,128)(2,1)S(1)} %collective-permute-done.p0), channel_id=1, source_target_pairs={{0,64},{16,80},{32,96},{48,112},{64,0},{80,16},{96,32},{112,48},{1... | collective-permute-start | bytes 245768 | tf_op jit(solution)/shard_map/ppermute | solution.py:27
  17.3 0.3 collective-permute-done.6.p2
  17.6 0.0 collective-permute-done.5.p1
  17.7 3.9 %collective-permute-start.8 = (bf16[1280,128]{1,0:T(8,128)(2,1)S(1)}, bf16[1280,128]{1,0:T(8,128)(2,1)S(1)}, u32[]{:S(2)}, u32[]{:S(2)}) collective-permute-start(bf16[1280,128]{1,0:T(8,128)(2,1)S(1)} %pad_maximum_fusion.1), channel_id=1, source_target_pairs={{0,16},{16,0},{32,48},{48,32},{64,80},{80,64},{96,112},{112,96},{1... | collective-permute-start | bytes 983048 | tf_op jit(solution)/shard_map/ppermute | solution.py:27
  21.5 0.0 collective-permute-done.3.p3
  21.6 0.1 collective-permute-done.2.p2
  21.7 0.0 collective-permute-done.1.p1
  21.7 2.1 %collective-permute-start.4 = (bf16[1280,128]{1,0:T(8,128)(2,1)S(1)}, bf16[1280,128]{1,0:T(8,128)(2,1)S(1)}, u32[]{:S(2)}, u32[]{:S(2)}) collective-permute-start(bf16[1280,128]{1,0:T(8,128)(2,1)S(1)} %pad_maximum_fusion), channel_id=1, source_target_pairs={{0,16},{16,0},{32,48},{48,32},{64,80},{80,64},{96,112},{112,96},{1... | collective-permute-start | bytes 983048 | tf_op jit(solution)/shard_map/ppermute | solution.py:27
  23.8 0.0 collective-permute-done.8.swapped
  23.8 0.0 slice-done
  23.8 0.0 slice-done.1
  23.8 0.0 slice-done.2
  23.8 0.0 slice-done.3
  23.8 0.0 slice-done.4
  23.8 0.0 copy-done
  23.9 4.1 %shard_map.51 = (bf16[128,2560]{1,0:T(8,128)(2,1)S(1)}, f32[2048,128]{1,0:T(8,128)S(1)}) custom-call(bf16[320,128]{1,0:T(8,128)(2,1)S(1)} %shard_map.50.p0, bf16[320,128]{1,0:T(8,128)(2,1)S(1)} %collective-permute-done.5.p1, bf16[320,128]{1,0:T(8,128)(2,1)S(1)} %collective-permute-done.6.p2, bf16[320,128]{1,0:T(8,128)(2,1)S(1)} %collective-permute-done.7.p3, ...), custom_call_target="tpu_custom_call" | custom-call | flops 1342177280 | bytes 8388608 | tf_op jit(solution)/shard_map/pallas_call | solution.py:139
  28.0 0.0 collective-permute-done.4.swapped
  28.0 5.0 %shard_map.52 = (bf16[128,5120]{1,0:T(8,128)(2,1)}, bf16[2048,128]{1,0:T(8,128)(2,1)}) custom-call(bf16[320,128]{1,0:T(8,128)(2,1)S(1)} %collective-permute-done.p0, bf16[320,128]{1,0:T(8,128)(2,1)S(1)} %collective-permute-done.1.p1, bf16[320,128]{1,0:T(8,128)(2,1)S(1)} %collective-permute-done.2.p2, bf16[320,128]{1,0:T(8,128)(2,1)S(1)} %collective-permute-done.3.p3, ...), custom_call_target="tpu_custom_call" | custom-call | flops 1342177280 | bytes 8388608 | tf_op jit(solution)/shard_map/pallas_call | solution.py:151
  (3 shorter events, 0.0 us)
Async XLA Ops:
  0.6 23.2 %slice-start = ((s8[20971520]{0:T(1024)(128)(4,1)}), s8[4194304]{0:T(1024)(128)(4,1)S(1)}, s32[]{:S(2)}) async-start(s8[20971520]{0:T(1024)(128)(4,1)} %bitcast.3), calls=%async_computation | async-start | bytes 8388608
  0.6 23.2 %slice-start.1 = ((s8[20971520]{0:T(1024)(128)(4,1)}), s8[4194304]{0:T(1024)(128)(4,1)S(1)}, s32[]{:S(2)}) async-start(s8[20971520]{0:T(1024)(128)(4,1)} %bitcast.3), calls=%async_computation.1 | async-start | bytes 8388608
  0.7 23.2 %slice-start.2 = ((s8[20971520]{0:T(1024)(128)(4,1)}), s8[4194304]{0:T(1024)(128)(4,1)S(1)}, s32[]{:S(2)}) async-start(s8[20971520]{0:T(1024)(128)(4,1)} %bitcast.3), calls=%async_computation.2 | async-start | bytes 8388608
  0.7 23.2 %slice-start.3 = ((s8[20971520]{0:T(1024)(128)(4,1)}), s8[4194304]{0:T(1024)(128)(4,1)S(1)}, s32[]{:S(2)}) async-start(s8[20971520]{0:T(1024)(128)(4,1)} %bitcast.3), calls=%async_computation.3 | async-start | bytes 8388608
  0.7 23.2 %slice-start.4 = ((s8[20971520]{0:T(1024)(128)(4,1)}), s8[4194304]{0:T(1024)(128)(4,1)S(1)}, s32[]{:S(2)}) async-start(s8[20971520]{0:T(1024)(128)(4,1)} %bitcast.3), calls=%async_computation.4 | async-start | bytes 8388608
  0.7 13.2 %collective-permute-start = (bf16[320,128]{1,0:T(8,128)(2,1)}, bf16[320,128]{1,0:T(8,128)(2,1)S(1)}, u32[]{:S(2)}, u32[]{:S(2)}) collective-permute-start(bf16[320,128]{1,0:T(8,128)(2,1)} %bitcast.8), channel_id=1, source_target_pairs={{0,128},{16,144},{32,160},{48,176},{64,192},{80,208},{96,224},{112... | collective-permute-start | bytes 245768 | tf_op jit(solution)/shard_map/ppermute | solution.py:27
  9.4 14.4 %copy-start = (bf16[1,128,5120]{2,1,0:T(8,128)(2,1)S(1)}, bf16[1,128,5120]{2,1,0:T(8,128)(2,1)}, u32[]{:S(2)}) copy-start(bf16[1,128,5120]{2,1,0:T(8,128)(2,1)} %param.4) | copy-start | bytes 3932164
  9.5 6.1 %collective-permute-start.7 = (bf16[320,128]{1,0:T(8,128)(2,1)S(1)}, bf16[320,128]{1,0:T(8,128)(2,1)S(1)}, u32[]{:S(2)}, u32[]{:S(2)}) collective-permute-start(bf16[320,128]{1,0:T(8,128)(2,1)S(1)} %shard_map.50.p0), channel_id=1, source_target_pairs={{0,96},{16,112},{32,0},{48,16},{64,32},{80,48},{96,64},{112,80},{1... | collective-permute-start | bytes 245768 | tf_op jit(solution)/shard_map/ppermute | solution.py:27
  12.3 5.4 %collective-permute-start.6 = (bf16[320,128]{1,0:T(8,128)(2,1)S(1)}, bf16[320,128]{1,0:T(8,128)(2,1)S(1)}, u32[]{:S(2)}, u32[]{:S(2)}) collective-permute-start(bf16[320,128]{1,0:T(8,128)(2,1)S(1)} %shard_map.50.p0), channel_id=1, source_target_pairs={{0,32},{16,48},{32,64},{48,80},{64,96},{80,112},{96,0},{112,16},{1... | collective-permute-start | bytes 245768 | tf_op jit(solution)/shard_map/ppermute | solution.py:27
  12.3 5.4 %collective-permute-start.5 = (bf16[320,128]{1,0:T(8,128)(2,1)S(1)}, bf16[320,128]{1,0:T(8,128)(2,1)S(1)}, u32[]{:S(2)}, u32[]{:S(2)}) collective-permute-start(bf16[320,128]{1,0:T(8,128)(2,1)S(1)} %shard_map.50.p0), channel_id=1, source_target_pairs={{0,64},{16,80},{32,96},{48,112},{64,0},{80,16},{96,32},{112,48},{1... | collective-permute-start | bytes 245768 | tf_op jit(solution)/shard_map/ppermute | solution.py:27
  13.9 7.6 %collective-permute-start.3 = (bf16[320,128]{1,0:T(8,128)(2,1)S(1)}, bf16[320,128]{1,0:T(8,128)(2,1)S(1)}, u32[]{:S(2)}, u32[]{:S(2)}) collective-permute-start(bf16[320,128]{1,0:T(8,128)(2,1)S(1)} %collective-permute-done.p0), channel_id=1, source_target_pairs={{0,96},{16,112},{32,0},{48,16},{64,32},{80,48},{96,64},{112,80},{1... | collective-permute-start | bytes 245768 | tf_op jit(solution)/shard_map/ppermute | solution.py:27
  15.0 6.7 %collective-permute-start.2 = (bf16[320,128]{1,0:T(8,128)(2,1)S(1)}, bf16[320,128]{1,0:T(8,128)(2,1)S(1)}, u32[]{:S(2)}, u32[]{:S(2)}) collective-permute-start(bf16[320,128]{1,0:T(8,128)(2,1)S(1)} %collective-permute-done.p0), channel_id=1, source_target_pairs={{0,32},{16,48},{32,64},{48,80},{64,96},{80,112},{96,0},{112,16},{1... | collective-permute-start | bytes 245768 | tf_op jit(solution)/shard_map/ppermute | solution.py:27
  15.5 6.2 %collective-permute-start.1 = (bf16[320,128]{1,0:T(8,128)(2,1)S(1)}, bf16[320,128]{1,0:T(8,128)(2,1)S(1)}, u32[]{:S(2)}, u32[]{:S(2)}) collective-permute-start(bf16[320,128]{1,0:T(8,128)(2,1)S(1)} %collective-permute-done.p0), channel_id=1, source_target_pairs={{0,64},{16,80},{32,96},{48,112},{64,0},{80,16},{96,32},{112,48},{1... | collective-permute-start | bytes 245768 | tf_op jit(solution)/shard_map/ppermute | solution.py:27
  17.7 6.1 %collective-permute-start.8 = (bf16[1280,128]{1,0:T(8,128)(2,1)S(1)}, bf16[1280,128]{1,0:T(8,128)(2,1)S(1)}, u32[]{:S(2)}, u32[]{:S(2)}) collective-permute-start(bf16[1280,128]{1,0:T(8,128)(2,1)S(1)} %pad_maximum_fusion.1), channel_id=1, source_target_pairs={{0,16},{16,0},{32,48},{48,32},{64,80},{80,64},{96,112},{112,96},{1... | collective-permute-start | bytes 983048 | tf_op jit(solution)/shard_map/ppermute | solution.py:27
  21.7 6.3 %collective-permute-start.4 = (bf16[1280,128]{1,0:T(8,128)(2,1)S(1)}, bf16[1280,128]{1,0:T(8,128)(2,1)S(1)}, u32[]{:S(2)}, u32[]{:S(2)}) collective-permute-start(bf16[1280,128]{1,0:T(8,128)(2,1)S(1)} %pad_maximum_fusion), channel_id=1, source_target_pairs={{0,16},{16,0},{32,48},{48,32},{64,80},{80,64},{96,112},{112,96},{1... | collective-permute-start | bytes 983048 | tf_op jit(solution)/shard_map/ppermute | solution.py:27

commit v3 on v0

v3 whole, which is shorter than its diff:
```python
import functools

import jax
import jax.numpy as jnp
from jax import lax
from jax.experimental import pallas as pl
from jax.experimental.pallas import tpu as pltpu
from jax.sharding import PartitionSpec as P

TILE = 128
EPSILON = 1e-06
TOKEN_BLOCK = 512
STEPS = (0, 2, 1, 3)
CHIP_COLUMNS = 5 * TILE
WHOLE = 2 * TILE
REST = 3 * TILE

NT = (((1,), (1,)), ((), ()))
VMEM = pl.BlockSpec(memory_space=pltpu.VMEM)
ANY = pl.BlockSpec(memory_space=pl.ANY)


def moved(dz=0, dy=0, dc=0):
    pairs = []
    for source in range(16):
        z, y, core = source >> 3, (source >> 1) & 3, source & 1
        pairs.append((source, ((z + dz) % 2) * 8 + ((y + dy) % 4) * 2 + (core + dc) % 2))
    return pairs


def send(value, **offset):
    return lax.ppermute(value, "replica", moved(**offset))


def anchor_kernel(out):
    out[...] = jnp.zeros_like(out)


def chip_start(slot, half_width):
    replica = lax.axis_index("replica")
    half, y = replica >> 3, (replica >> 1) & 3
    chip = lax.rem(y + 4 - STEPS[slot % 4], 4)
    side = half if slot < 4 else 1 - half
    return side * half_width + chip * CHIP_COLUMNS


def renew(delta_tiles, starts, width, held, weights, renewed, sems):
    row = lax.broadcasted_iota(jnp.int32, (TILE, TILE), 0)
    col = lax.broadcasted_iota(jnp.int32, (TILE, TILE), 1)
    identity = (row == col).astype(jnp.bfloat16)
    copies = []
    for slot, start in enumerate(starts):
        for t in range(width // TILE):
            tile = delta_tiles(slot, t).astype(jnp.float32)
            scale = jnp.max(jnp.abs(tile), axis=(0, 1), keepdims=True) + EPSILON
            normalized = (tile / scale).astype(jnp.bfloat16)
            turned = lax.dot_general(identity, normalized, NT, preferred_element_type=jnp.float32)
            columns = pl.ds(pl.multiple_of(start + t * TILE, TILE), TILE)
            fresh = held[:, columns].astype(jnp.float32) + turned * scale
            at = slot * width + t * TILE
            weights[:, at : at + TILE] = fresh.astype(jnp.bfloat16)
        copies.append(
            pltpu.make_async_copy(
                weights.at[:, pl.ds(slot * width, width)],
                renewed.at[:, pl.ds(pl.multiple_of(start, TILE), width)],
                sems.at[slot],
            )
        )
        copies[-1].start()
    return copies


def products(starts, width, tokens, weights):
    for block in range(tokens.shape[0] // TOKEN_BLOCK):
        rows = pl.ds(block * TOKEN_BLOCK, TOKEN_BLOCK)
        left = jnp.concatenate(
            [tokens[rows, pl.ds(pl.multiple_of(start, TILE), width)] for start in starts], axis=1
        )
        yield block, rows, lax.dot_general(left, weights[...], NT, preferred_element_type=jnp.float32)


def whole_kernel(slots, first, *refs):
    pieces, (held, tokens, before), refs = refs[: len(slots)], refs[len(slots) : len(slots) + 3], refs[len(slots) + 3 :]
    if not first:
        refs = refs[1:]
    renewed, total, weights, sems = refs
    core = lax.axis_index("replica") & 1
    starts = [chip_start(slot, tokens.shape[1] // 2) + core * REST for slot in slots]

    def delta_tiles(index, t):
        return pieces[index][pl.ds(pl.multiple_of(core * (TILE // 2) + t * TILE, TILE // 2), TILE), :]

    copies = renew(delta_tiles, starts, WHOLE, held, weights, renewed, sems)
    for _, rows, product in products(starts, WHOLE, tokens, weights):
        total[rows, :] = product if first else before[rows, :] + product
    for copy in copies:
        copy.wait()


def rest_kernel(slots, *refs):
    count = len(slots)
    pieces, (others, held, tokens, before, _) = refs[:count], refs[count : count + 5]
    renewed, result, delta, weights, result_block, sems, result_sems = refs[count + 5 :]
    core = lax.axis_index("replica") & 1
    rows_each = pieces[0].shape[0]
    half_tile = TILE // 2
    starts = [chip_start(slot, tokens.shape[1] // 2) + (1 - core) * WHOLE for slot in slots]
    for index in range(count):
        own_to = pl.multiple_of(index * REST + core * rows_each, half_tile)
        other_to = pl.multiple_of(index * REST + (1 - core) * half_tile, half_tile)
        own_from = pl.multiple_of((1 - core) * WHOLE, half_tile)
        delta[pl.ds(own_to, half_tile), :] = pieces[index][pl.ds(own_from, half_tile), :]
        delta[pl.ds(other_to, rows_each), :] = others[index * rows_each : (index + 1) * rows_each, :]

    def delta_tiles(index, t):
        return delta[index * REST + t * TILE : index * REST + (t + 1) * TILE, :]

    copies = renew(delta_tiles, starts, REST, held, weights, renewed, sems)
    for block, rows, product in products(starts, REST, tokens, weights):
        result_block[rows, :] = (before[rows, :] + product).astype(jnp.bfloat16)
        copies.append(
            pltpu.make_async_copy(result_block.at[rows, :], result.at[rows, :], result_sems.at[block])
        )
        copies[-1].start()
    for copy in copies:
        copy.wait()


def call_kernel(kernel, operands, specs, total, total_spec, aliases, scratch, held, tokens, width):
    return pl.pallas_call(
        kernel,
        out_shape=(jax.ShapeDtypeStruct((held.shape[0], tokens.shape[1]), jnp.bfloat16), total),
        in_specs=specs,
        out_specs=(ANY, total_spec),
        scratch_shapes=scratch,
        input_output_aliases=aliases,
        compiler_params=pltpu.CompilerParams(vmem_limit_bytes=12 * 2**20),
        cost_estimate=pl.CostEstimate(
            flops=4 * tokens.shape[0] * held.shape[0] * width, bytes_accessed=2 * 2**20, transcendentals=0
        ),
    )(*operands)


def whole_part(slots, pieces, held, tokens, before):
    first = not isinstance(before, (tuple, list))
    width = len(slots) * WHOLE
    operands = [*pieces, held, tokens]
    specs = [VMEM] * len(operands)
    aliases = {}
    if first:
        operands.append(before)
        specs.append(ANY)
    else:
        renewed, partial = before
        operands += [partial, renewed]
        specs += [VMEM, ANY]
        aliases = {len(operands) - 2: 1, len(operands) - 1: 0}
    scratch = [
        pltpu.VMEM((held.shape[0], width), jnp.bfloat16),
        pltpu.SemaphoreType.DMA((len(slots),)),
    ]
    total = pltpu.VMEM((tokens.shape[0], held.shape[0]), jnp.float32)
    kernel = functools.partial(whole_kernel, slots, first)
    return call_kernel(kernel, operands, specs, total, VMEM, aliases, scratch, held, tokens, width)


def rest_part(slots, pieces, others, held, tokens, before):
    renewed, partial = before
    width = len(slots) * REST
    operands = [*pieces, others, held, tokens, partial, renewed]
    specs = [VMEM] * (len(operands) - 1) + [ANY]
    scratch = [
        pltpu.VMEM((width, held.shape[0]), jnp.bfloat16),
        pltpu.VMEM((held.shape[0], width), jnp.bfloat16),
        pltpu.VMEM((tokens.shape[0], held.shape[0]), jnp.bfloat16),
        pltpu.SemaphoreType.DMA((len(slots),)),
        pltpu.SemaphoreType.DMA((tokens.shape[0] // TOKEN_BLOCK,)),
    ]
    total = jax.ShapeDtypeStruct((tokens.shape[0], held.shape[0]), jnp.bfloat16)
    kernel = functools.partial(rest_kernel, slots)
    return call_kernel(
        kernel, operands, specs, total, ANY, {len(operands) - 1: 0}, scratch, held, tokens, width
    )


def on_device(weight_delta, rollout_copy, cached_inputs):
    piece = weight_delta.T
    tokens = pltpu.with_memory_space_constraint(cached_inputs, pltpu.VMEM)
    held = pltpu.with_memory_space_constraint(rollout_copy[0], pltpu.VMEM)

    anchor = pl.pallas_call(
        anchor_kernel,
        out_shape=pltpu.VMEM((8, 128), jnp.float32),
        out_specs=VMEM,
        compiler_params=pltpu.CompilerParams(vmem_limit_bytes=2**20),
        cost_estimate=pl.CostEstimate(flops=10**10, bytes_accessed=24 * 2**20, transcendentals=0),
    )()
    own, anchor = lax.optimization_barrier((piece, anchor))
    far_piece = send(piece, dz=1)
    near = [own] + [send(own, dy=step) for step in STEPS[1:]]
    far = [far_piece] + [send(far_piece, dy=step) for step in STEPS[1:]]
    done = whole_part((0, 1, 2, 3), near, held, tokens, anchor)
    near, far, done = lax.optimization_barrier((near, far, done))
    others = send(jnp.concatenate(near + far), dc=1)
    done = whole_part((4, 5, 6, 7), far, held, tokens, done)
    renewed, result = rest_part(tuple(range(8)), near + far, others, held, tokens, done)
    return (renewed[None], result)


def solution(mesh):
    placed = (P("tp", "replica"), P("replica", "tp", None), P("replica", None))
    return jax.shard_map(
        on_device,
        mesh=mesh,
        in_specs=placed,
        out_specs=(P("replica", "tp", None), P("replica", "tp")),
        check_vma=False,
    )
```

time: 144 us -> 30.3 us (0.21)
  waiting for transfers between devices: 58.1 us -> 2.45 us
  blocking collectives: 45.6 us -> 0 us
  starting transfers between devices: 0.04 us -> 17.9 us
  matrix products: 13.4 us -> 0 us
  between operations: 14.1 us -> 0.89 us
  Pallas kernels: 0 us -> 8.81 us
  other arithmetic: 6.97 us -> 0 us
  local copies, waits for them, and re-layouts: 5.19 us -> 0.13 us
    all_gather x1 -> x0, waiting for transfers between devices: 58.1 us -> none  [on_device(): block_piece = lax.all_gather(payload, 'replica', axis=1, tiled=True)]
    pmax x1 -> x0, blocking collectives: 45.6 us -> none  [on_device(): tile_scale = lax.pmax(partial_max, 'replica') + EPSILON]
    ppermute x0 -> x8, starting transfers between devices: none -> 17.9 us  [send(): return lax.ppermute(value, 'replica', moved(**offset))]
    dot_general x3 -> x0, matrix products: 13.4 us -> none  [the longest x1 12.7 us: project_rows(): lax.dot_general(token_rows, weights, (((1,), (1,)), ((), ())), preferred_...]
    pallas_call x0 -> x4, Pallas kernels: none -> 8.81 us  [the longest x3 8.81 us: call_kernel(): pl.pallas_call(kernel, out_shape=(jax.ShapeDtypeStruct((held.shape[0], to...]
    unnamed x5 -> x13, local copies, waits for them, and re-layouts: 5.19 us -> 0.11 us
    broadcast_in_dim x1 -> x0, other arithmetic: 4.2 us -> none  [on_device(): return (fresh_block[None], running.astype(jnp.bfloat16))]
    ppermute x0 -> x8, waiting for transfers between devices: none -> 2.45 us  [send(): return lax.ppermute(value, 'replica', moved(**offset))]
  transfers between devices with their start and end apart: 1 -> 8, of which waited for: 1 -> 2; matrix products, arithmetic and copies ran while one was open for 1% -> 0% of each run, Pallas kernels for 0% -> 12%
where the time goes in v3:
time: 30.3 us; the launch traced here: 30.2 us
  starting transfers between devices  17.9 us (59%)
  Pallas kernels  8.81 us (29%)
  waiting for transfers between devices  2.45 us (8%)
  between operations  0.89 us (3%)
    ppermute x8, starting transfers between devices, send(): return lax.ppermute(value, 'replica', moved(**offset))  17.9 us
    pallas_call x3, Pallas kernels, call_kernel(): pl.pallas_call(kernel, out_shape=(jax.ShapeDtypeStruct((held.shape[0], to...  8.81 us
    ppermute x8, waiting for transfers between devices, send(): return lax.ppermute(value, 'replica', moved(**offset))  2.45 us
  transfers between devices with their start and end apart: 8, of which 2 were waited for; matrix products, arithmetic and copies ran while one was open for 0% of the time, Pallas kernels for 12%

profile of v3, /device:TPU:1, one launch (start us, length us, event | category | flops | bytes accessed | tf_op | source)
XLA Modules:
  0.0 30.2 jit_solution(17057729694207533138)
XLA Ops:
  0.6 0.0 copy-start.2
  0.6 0.0 copy-start.1
  0.6 7.8 %collective-permute-start.3 = (bf16[320,128]{1,0:T(8,128)(2,1)}, bf16[320,128]{1,0:T(8,128)(2,1)S(1)}, u32[]{:S(2)}, u32[]{:S(2)}) collective-permute-start(bf16[320,128]{1,0:T(8,128)(2,1)} %bitcast.6), channel_id=1, source_target_pairs={{0,128},{16,144},{32,160},{48,176},{64,192},{80,208},{96,224},{112... | collective-permute-start | bytes 245768 | tf_op jit(solution)/shard_map/ppermute | solution.py:32
  8.5 0.0 copy-start
  8.5 0.0 copy-done.2
  8.5 2.7 %collective-permute-start.2 = (bf16[320,128]{1,0:T(8,128)(2,1)S(1)}, bf16[320,128]{1,0:T(8,128)(2,1)S(1)}, u32[]{:S(2)}, u32[]{:S(2)}) collective-permute-start(bf16[320,128]{1,0:T(8,128)(2,1)S(1)} %bitcast.7), channel_id=1, source_target_pairs={{0,96},{16,112},{32,0},{48,16},{64,32},{80,48},{96,64},{112,80},{1... | collective-permute-start | bytes 245768 | tf_op jit(solution)/shard_map/ppermute | solution.py:32
  11.2 0.0 collective-permute-start.1
  11.2 1.6 %collective-permute-start = (bf16[320,128]{1,0:T(8,128)(2,1)S(1)}, bf16[320,128]{1,0:T(8,128)(2,1)S(1)}, u32[]{:S(2)}, u32[]{:S(2)}) collective-permute-start(bf16[320,128]{1,0:T(8,128)(2,1)S(1)} %bitcast.9), channel_id=1, source_target_pairs={{0,64},{16,80},{32,96},{48,112},{64,0},{80,16},{96,32},{112,48},{1... | collective-permute-start | bytes 245768 | tf_op jit(solution)/shard_map/ppermute | solution.py:32
  12.9 0.0 collective-permute-done.3.refs_0_.refs_4_
  12.9 1.0 %collective-permute-start.6 = (bf16[320,128]{1,0:T(8,128)(2,1)S(1)}, bf16[320,128]{1,0:T(8,128)(2,1)S(1)}, u32[]{:S(2)}, u32[]{:S(2)}) collective-permute-start(bf16[320,128]{1,0:T(8,128)(2,1)S(1)} %collective-permute-done.3.refs_0_.refs_4_), channel_id=1, source_target_pairs={{0,96},{16,112},{32,0},{48,16},{64,32},{80,48},{96,64},{112,80},{1... | collective-permute-start | bytes 245768 | tf_op jit(solution)/shard_map/ppermute | solution.py:32
  13.9 0.6 %collective-permute-start.5 = (bf16[320,128]{1,0:T(8,128)(2,1)S(1)}, bf16[320,128]{1,0:T(8,128)(2,1)S(1)}, u32[]{:S(2)}, u32[]{:S(2)}) collective-permute-start(bf16[320,128]{1,0:T(8,128)(2,1)S(1)} %collective-permute-done.3.refs_0_.refs_4_), channel_id=1, source_target_pairs={{0,32},{16,48},{32,64},{48,80},{64,96},{80,112},{96,0},{112,16},{1... | collective-permute-start | bytes 245768 | tf_op jit(solution)/shard_map/ppermute | solution.py:32
  14.5 0.0 collective-permute-done.2.refs_3_
  14.5 1.8 %collective-permute-start.4 = (bf16[320,128]{1,0:T(8,128)(2,1)S(1)}, bf16[320,128]{1,0:T(8,128)(2,1)S(1)}, u32[]{:S(2)}, u32[]{:S(2)}) collective-permute-start(bf16[320,128]{1,0:T(8,128)(2,1)S(1)} %collective-permute-done.3.refs_0_.refs_4_), channel_id=1, source_target_pairs={{0,64},{16,80},{32,96},{48,112},{64,0},{80,16},{96,32},{112,48},{1... | collective-permute-start | bytes 245768 | tf_op jit(solution)/shard_map/ppermute | solution.py:32
  16.3 0.3 collective-permute-done.1.refs_2_
  16.6 0.0 collective-permute-done.refs_1_
  16.6 0.0 copy-done.1
  16.6 0.0 copy-done
  16.6 1.9 %shard_map.51 = (bf16[128,5120]{1,0:T(8,128)(2,1)}, f32[2048,128]{1,0:T(8,128)S(1)}) custom-call(bf16[320,128]{1,0:T(8,128)(2,1)S(1)} %bitcast.10, bf16[320,128]{1,0:T(8,128)(2,1)S(1)} %collective-permute-done.refs_1_, bf16[320,128]{1,0:T(8,128)(2,1)S(1)} %collective-permute-done.1.refs_2_, bf16[320,128]{1,0:T(8,128)(2,1)S(1)} %collective-permute-done.2.refs_3_, ...), custom_call_target="tpu_custom_call" | custom-call | flops 1073741824 | bytes 2097152 | tf_op jit(solution)/shard_map/pallas_call | solution.py:130
  18.5 0.0 collective-permute-done.6.refs_3_.refs_7_
  18.5 2.1 %collective-permute-done.5.refs_2_.refs_6_ = bf16[320,128]{1,0:T(8,128)(2,1)S(1)} collective-permute-done((bf16[320,128]{1,0:T(8,128)(2,1)S(1)}, bf16[320,128]{1,0:T(8,128)(2,1)S(1)}, u32[]{:S(2)}, u32[]{:S(2)}) %collective-permute-start.5) | collective-permute-done | bytes 81952 | tf_op jit(solution)/shard_map/ppermute | solution.py:32
  20.6 0.0 collective-permute-done.4.refs_1_.refs_5_
  20.7 2.3 %collective-permute-start.7 = (bf16[2560,128]{1,0:T(8,128)(2,1)S(1)}, bf16[2560,128]{1,0:T(8,128)(2,1)S(1)}, u32[]{:S(2)}, u32[]{:S(2)}) collective-permute-start(bf16[2560,128]{1,0:T(8,128)(2,1)S(1)} %constant_dynamic-update-slice_fusion), channel_id=1, source_target_pairs={{0,16},{16,0},{32,48},{48,32},{64,80},{80,64},{96,112},{112,96},{1... | collective-permute-start | bytes 1966088 | tf_op jit(solution)/shard_map/ppermute | solution.py:32
  23.1 1.8 %shard_map.52 = (bf16[128,5120]{1,0:T(8,128)(2,1)}, f32[2048,128]{1,0:T(8,128)S(1)}) custom-call(bf16[320,128]{1,0:T(8,128)(2,1)S(1)} %collective-permute-done.3.refs_0_.refs_4_, bf16[320,128]{1,0:T(8,128)(2,1)S(1)} %collective-permute-done.4.refs_1_.refs_5_, ...), custom_call_target="tpu_custom_call", output_to_operand_aliasing={{1}: (6, {}), {0}: (7, {})} | custom-call | flops 1073741824 | bytes 2097152 | tf_op jit(solution)/shard_map/pallas_call | solution.py:130
  24.8 0.0 collective-permute-done.7.refs_8_
  24.9 5.2 %shard_map.53 = (bf16[128,5120]{1,0:T(8,128)(2,1)}, bf16[2048,128]{1,0:T(8,128)(2,1)}) custom-call(bf16[320,128]{1,0:T(8,128)(2,1)S(1)} %bitcast.12, bf16[320,128]{1,0:T(8,128)(2,1)S(1)} %collective-permute-done.refs_1_, bf16[320,128]{1,0:T(8,128)(2,1)S(1)} %collective-permute-done.1.refs_2_, ...), custom_call_target="tpu_custom_call", output_to_operand_aliasing={{0}: (12, {})} | custom-call | flops 3221225472 | bytes 2097152 | tf_op jit(solution)/shard_map/pallas_call | solution.py:130
  (9 shorter events, 0.1 us)
Async XLA Ops:
  0.6 7.9 %copy-start.2 = (bf16[128,320]{0,1:T(8,128)(2,1)S(1)}, bf16[128,320]{0,1:T(8,128)(2,1)}, u32[]{:S(2)}) copy-start(bf16[128,320]{0,1:T(8,128)(2,1)} %param.3) | copy-start | bytes 245764
  0.6 16.0 %copy-start.1 = (bf16[1,128,5120]{2,1,0:T(8,128)(2,1)S(1)}, bf16[1,128,5120]{2,1,0:T(8,128)(2,1)}, u32[]{:S(2)}) copy-start(bf16[1,128,5120]{2,1,0:T(8,128)(2,1)} %param.4) | copy-start | bytes 3932164
  0.6 12.2 %collective-permute-start.3 = (bf16[320,128]{1,0:T(8,128)(2,1)}, bf16[320,128]{1,0:T(8,128)(2,1)S(1)}, u32[]{:S(2)}, u32[]{:S(2)}) collective-permute-start(bf16[320,128]{1,0:T(8,128)(2,1)} %bitcast.6), channel_id=1, source_target_pairs={{0,128},{16,144},{32,160},{48,176},{64,192},{80,208},{96,224},{112... | collective-permute-start | bytes 245768 | tf_op jit(solution)/shard_map/ppermute | solution.py:32
  8.5 8.1 %copy-start = (bf16[2048,5120]{1,0:T(8,128)(2,1)S(1)}, bf16[2048,5120]{1,0:T(8,128)(2,1)}, u32[]{:S(2)}) copy-start(bf16[2048,5120]{1,0:T(8,128)(2,1)} %refs_10_.1) | copy-start | bytes 62914564
  8.5 6.0 %collective-permute-start.2 = (bf16[320,128]{1,0:T(8,128)(2,1)S(1)}, bf16[320,128]{1,0:T(8,128)(2,1)S(1)}, u32[]{:S(2)}, u32[]{:S(2)}) collective-permute-start(bf16[320,128]{1,0:T(8,128)(2,1)S(1)} %bitcast.7), channel_id=1, source_target_pairs={{0,96},{16,112},{32,0},{48,16},{64,32},{80,48},{96,64},{112,80},{1... | collective-permute-start | bytes 245768 | tf_op jit(solution)/shard_map/ppermute | solution.py:32
  11.2 5.4 %collective-permute-start.1 = (bf16[320,128]{1,0:T(8,128)(2,1)S(1)}, bf16[320,128]{1,0:T(8,128)(2,1)S(1)}, u32[]{:S(2)}, u32[]{:S(2)}) collective-permute-start(bf16[320,128]{1,0:T(8,128)(2,1)S(1)} %bitcast.8), channel_id=1, source_target_pairs={{0,32},{16,48},{32,64},{48,80},{64,96},{80,112},{96,0},{112,16},{1... | collective-permute-start | bytes 245768 | tf_op jit(solution)/shard_map/ppermute | solution.py:32
  11.2 5.4 %collective-permute-start = (bf16[320,128]{1,0:T(8,128)(2,1)S(1)}, bf16[320,128]{1,0:T(8,128)(2,1)S(1)}, u32[]{:S(2)}, u32[]{:S(2)}) collective-permute-start(bf16[320,128]{1,0:T(8,128)(2,1)S(1)} %bitcast.9), channel_id=1, source_target_pairs={{0,64},{16,80},{32,96},{48,112},{64,0},{80,16},{96,32},{112,48},{1... | collective-permute-start | bytes 245768 | tf_op jit(solution)/shard_map/ppermute | solution.py:32
  12.9 5.6 %collective-permute-start.6 = (bf16[320,128]{1,0:T(8,128)(2,1)S(1)}, bf16[320,128]{1,0:T(8,128)(2,1)S(1)}, u32[]{:S(2)}, u32[]{:S(2)}) collective-permute-start(bf16[320,128]{1,0:T(8,128)(2,1)S(1)} %collective-permute-done.3.refs_0_.refs_4_), channel_id=1, source_target_pairs={{0,96},{16,112},{32,0},{48,16},{64,32},{80,48},{96,64},{112,80},{1... | collective-permute-start | bytes 245768 | tf_op jit(solution)/shard_map/ppermute | solution.py:32
  13.9 6.7 %collective-permute-start.5 = (bf16[320,128]{1,0:T(8,128)(2,1)S(1)}, bf16[320,128]{1,0:T(8,128)(2,1)S(1)}, u32[]{:S(2)}, u32[]{:S(2)}) collective-permute-start(bf16[320,128]{1,0:T(8,128)(2,1)S(1)} %collective-permute-done.3.refs_0_.refs_4_), channel_id=1, source_target_pairs={{0,32},{16,48},{32,64},{48,80},{64,96},{80,112},{96,0},{112,16},{1... | collective-permute-start | bytes 245768 | tf_op jit(solution)/shard_map/ppermute | solution.py:32
  14.5 6.1 %collective-permute-start.4 = (bf16[320,128]{1,0:T(8,128)(2,1)S(1)}, bf16[320,128]{1,0:T(8,128)(2,1)S(1)}, u32[]{:S(2)}, u32[]{:S(2)}) collective-permute-start(bf16[320,128]{1,0:T(8,128)(2,1)S(1)} %collective-permute-done.3.refs_0_.refs_4_), channel_id=1, source_target_pairs={{0,64},{16,80},{32,96},{48,112},{64,0},{80,16},{96,32},{112,48},{1... | collective-permute-start | bytes 245768 | tf_op jit(solution)/shard_map/ppermute | solution.py:32
  20.7 4.1 %collective-permute-start.7 = (bf16[2560,128]{1,0:T(8,128)(2,1)S(1)}, bf16[2560,128]{1,0:T(8,128)(2,1)S(1)}, u32[]{:S(2)}, u32[]{:S(2)}) collective-permute-start(bf16[2560,128]{1,0:T(8,128)(2,1)S(1)} %constant_dynamic-update-slice_fusion), channel_id=1, source_target_pairs={{0,16},{16,0},{32,48},{48,32},{64,80},{80,64},{96,112},{112,96},{1... | collective-permute-start | bytes 1966088 | tf_op jit(solution)/shard_map/ppermute | solution.py:32

commit v4 on v3

v4 whole, which is shorter than its diff:
```python
import functools

import jax
import jax.numpy as jnp
from jax import lax
from jax.experimental import pallas as pl
from jax.experimental.pallas import tpu as pltpu
from jax.sharding import PartitionSpec as P

TILE = 128
EPSILON = 1e-06
TOKEN_BLOCK = 512
STEPS = ((0, 0), (1, 2), (2, 1), (3, 3))
OTHER_SLOT = (0, 2, 1, 3)
CHIP_COLUMNS = 5 * TILE
WHOLE = 2 * TILE
REST = 3 * TILE

NT = (((1,), (1,)), ((), ()))
VMEM = pl.BlockSpec(memory_space=pltpu.VMEM)
ANY = pl.BlockSpec(memory_space=pl.ANY)


def moved(dz=0, dy=(0, 0), dc=0):
    pairs = []
    for source in range(16):
        z, y, core = source >> 3, (source >> 1) & 3, source & 1
        pairs.append((source, (z ^ dz) * 8 + (y ^ dy[core]) * 2 + (core ^ dc)))
    return pairs


def send(value, **offset):
    return lax.ppermute(value, "replica", moved(**offset))


def anchor_kernel(out):
    out[...] = jnp.zeros_like(out)


def chip_start(slot, far, half_width):
    replica = lax.axis_index("replica")
    half, y = replica >> 3, (replica >> 1) & 3
    step = STEPS[slot]
    chip = y ^ (step[0] + (replica & 1) * (step[1] - step[0]))
    side = 1 - half if far else half
    return side * half_width + chip * CHIP_COLUMNS


def renew(delta, spans, held, weights, renewed, sems):
    row = lax.broadcasted_iota(jnp.int32, (TILE, TILE), 0)
    col = lax.broadcasted_iota(jnp.int32, (TILE, TILE), 1)
    identity = (row == col).astype(jnp.bfloat16)
    copies, at = [], 0
    for slot, (start, width) in enumerate(spans):
        for t in range(width // TILE):
            tile = delta[at + t * TILE : at + (t + 1) * TILE, :].astype(jnp.float32)
            scale = jnp.max(jnp.abs(tile), axis=(0, 1), keepdims=True) + EPSILON
            normalized = (tile / scale).astype(jnp.bfloat16)
            turned = lax.dot_general(identity, normalized, NT, preferred_element_type=jnp.float32)
            columns = pl.ds(pl.multiple_of(start + t * TILE, TILE), TILE)
            fresh = held[:, columns].astype(jnp.float32) + turned * scale
            weights[:, at + t * TILE : at + (t + 1) * TILE] = fresh.astype(jnp.bfloat16)
        copies.append(
            pltpu.make_async_copy(
                weights.at[:, pl.ds(at, width)],
                renewed.at[:, pl.ds(pl.multiple_of(start, TILE), width)],
                sems.at[slot],
            )
        )
        copies[-1].start()
        at += width
    return copies


def products(spans, tokens, weights):
    for block in range(tokens.shape[0] // TOKEN_BLOCK):
        rows = pl.ds(block * TOKEN_BLOCK, TOKEN_BLOCK)
        left = jnp.concatenate(
            [tokens[rows, pl.ds(pl.multiple_of(start, TILE), width)] for start, width in spans], axis=1
        )
        yield block, rows, lax.dot_general(left, weights[...], NT, preferred_element_type=jnp.float32)


def place_whole(delta, at, core, mine):
    delta[at : at + WHOLE, :] = jnp.where(core == 0, mine[:WHOLE, :], mine[TILE // 2 :, :])


def place_rest(delta, at, core, mine, other):
    end, half_tile = at + REST, TILE // 2
    delta[at : at + half_tile, :] = jnp.where(core == 0, mine[WHOLE:, :], other[:half_tile, :])
    delta[at + half_tile : end - half_tile, :] = jnp.where(
        core == 0, other[: WHOLE, :], other[half_tile:, :]
    )
    delta[end - half_tile : end, :] = jnp.where(core == 0, other[WHOLE:, :], mine[:half_tile, :])


def add_products(first, spans, tokens, weights, before, total):
    for _, rows, product in products(spans, tokens, weights):
        total[rows, :] = product if first else before[rows, :] + product


def whole_kernel(slots, first, *refs):
    count = len(slots)
    pieces, (held, tokens, before), refs = refs[:count], refs[count : count + 3], refs[count + 3 :]
    renewed, total, delta, weights, sems = refs[-5:]
    core = lax.axis_index("replica") & 1
    spans = []
    for index, slot in enumerate(slots):
        place_whole(delta, index * WHOLE, core, pieces[index][...])
        spans.append((chip_start(slot % 4, slot >= 4, tokens.shape[1] // 2) + core * REST, WHOLE))
    copies = renew(delta, spans, held, weights, renewed, sems)
    add_products(first, spans, tokens, weights, before, total)
    for copy in copies:
        copy.wait()


def rest_kernel(slots, last, *refs):
    count = len(slots)
    pieces, (others, held, tokens, before, _), refs = refs[:count], refs[count : count + 5], refs[count + 5 :]
    renewed, total, delta, weights = refs[:4]
    sems = refs[5 if last else 4]
    core = lax.axis_index("replica") & 1
    rows = pieces[0].shape[0]
    spans = []
    for index, slot in enumerate(slots):
        other = index - slot % 4 + OTHER_SLOT[slot % 4]
        place_rest(delta, index * REST, core, pieces[index][...], others[other * rows : (other + 1) * rows, :])
        spans.append((chip_start(slot % 4, slot >= 4, tokens.shape[1] // 2) + (1 - core) * WHOLE, REST))
    copies = renew(delta, spans, held, weights, renewed, sems)
    for block, rows, product in products(spans, tokens, weights):
        if not last:
            total[rows, :] = before[rows, :] + product
            continue
        result_block, result_sems = refs[4], refs[6]
        result_block[rows, :] = (before[rows, :] + product).astype(jnp.bfloat16)
        copies.append(
            pltpu.make_async_copy(result_block.at[rows, :], total.at[rows, :], result_sems.at[block])
        )
        copies[-1].start()
    for copy in copies:
        copy.wait()


def whole_part(slots, pieces, held, tokens, before):
    first = not isinstance(before, (tuple, list))
    kernel = functools.partial(whole_kernel, slots, first)
    return run_kernel(kernel, pieces, held, tokens, before, 2 * len(slots), len(slots))


def rest_part(slots, pieces, others, held, tokens, before, last=False):
    kernel = functools.partial(rest_kernel, slots, last)
    return run_kernel(kernel, [*pieces, others], held, tokens, before, 3 * len(slots), len(slots), last)


def run_kernel(kernel, pieces, held, tokens, before, tiles, span_count, last=False):
    width = tiles * TILE
    token_count, row_count = tokens.shape[0], held.shape[0]
    operands = [*pieces, held, tokens]
    specs = [VMEM] * len(operands)
    aliases = {}
    if isinstance(before, (tuple, list)):
        renewed, partial = before
        operands += [partial, renewed]
        specs += [VMEM, ANY]
        aliases = {len(operands) - 1: 0}
        if not last:
            aliases[len(operands) - 2] = 1
    else:
        operands.append(before)
        specs.append(ANY)
    scratch = [
        pltpu.VMEM((width, row_count), jnp.bfloat16),
        pltpu.VMEM((row_count, width), jnp.bfloat16),
    ]
    if last:
        total, total_spec = jax.ShapeDtypeStruct((token_count, row_count), jnp.bfloat16), ANY
        scratch.append(pltpu.VMEM((token_count, row_count), jnp.bfloat16))
    else:
        total, total_spec = pltpu.VMEM((token_count, row_count), jnp.float32), VMEM
    scratch.append(pltpu.SemaphoreType.DMA((span_count,)))
    if last:
        scratch.append(pltpu.SemaphoreType.DMA((token_count // TOKEN_BLOCK,)))
    return pl.pallas_call(
        kernel,
        out_shape=(jax.ShapeDtypeStruct((row_count, tokens.shape[1]), jnp.bfloat16), total),
        in_specs=specs,
        out_specs=(ANY, total_spec),
        scratch_shapes=scratch,
        input_output_aliases=aliases,
        compiler_params=pltpu.CompilerParams(vmem_limit_bytes=12 * 2**20),
        cost_estimate=pl.CostEstimate(
            flops=4 * token_count * row_count * width, bytes_accessed=2 * 2**20, transcendentals=0
        ),
    )(*operands)


def on_device(weight_delta, rollout_copy, cached_inputs):
    piece = weight_delta.T
    tokens = pltpu.with_memory_space_constraint(cached_inputs, pltpu.VMEM)
    held = pltpu.with_memory_space_constraint(rollout_copy[0], pltpu.VMEM)

    anchor = pl.pallas_call(
        anchor_kernel,
        out_shape=pltpu.VMEM((8, 128), jnp.float32),
        out_specs=VMEM,
        compiler_params=pltpu.CompilerParams(vmem_limit_bytes=2**20),
        cost_estimate=pl.CostEstimate(flops=10**10, bytes_accessed=24 * 2**20, transcendentals=0),
    )()
    own, anchor = lax.optimization_barrier((piece, anchor))
    far_piece = send(piece, dz=1)
    near = [own] + [send(own, dy=step) for step in STEPS[1:]]
    far = [far_piece] + [send(far_piece, dy=step) for step in STEPS[1:]]
    done = whole_part((0, 1, 2, 3, 4), near + far[:1], held, tokens, anchor)
    near, far, done = lax.optimization_barrier((near, far, done))
    others = send(jnp.concatenate(near + far), dc=1)
    done = whole_part((5, 6, 7), far[1:], held, tokens, done)
    renewed, result = rest_part(tuple(range(8)), near + far, others, held, tokens, done, last=True)
    return (renewed[None], result)


def solution(mesh):
    placed = (P("tp", "replica"), P("replica", "tp", None), P("replica", None))
    return jax.shard_map(
        on_device,
        mesh=mesh,
        in_specs=placed,
        out_specs=(P("replica", "tp", None), P("replica", "tp")),
        check_vma=False,
    )
```

time: 30.3 us -> 29.8 us (0.983)
  transfers between devices with their start and end apart: 8 -> 8, of which waited for: 2 -> 3; matrix products, arithmetic and copies ran while one was open for 0% -> 0% of each run, Pallas kernels for 12% -> 12%
where the time goes in v4:
time: 29.8 us; the launch traced here: 29.7 us
  starting transfers between devices  18 us (60%)
  Pallas kernels  8.7 us (29%)
  waiting for transfers between devices  2.19 us (7%)
  between operations  0.72 us (2%)
    ppermute x8, starting transfers between devices, send(): return lax.ppermute(value, 'replica', moved(**offset))  18 us
    pallas_call x3, Pallas kernels, run_kernel(): pl.pallas_call(kernel, out_shape=(jax.ShapeDtypeStruct((row_count, tokens...  8.7 us
    ppermute x8, waiting for transfers between devices, send(): return lax.ppermute(value, 'replica', moved(**offset))  2.19 us
  transfers between devices with their start and end apart: 8, of which 3 were waited for; matrix products, arithmetic and copies ran while one was open for 0% of the time, Pallas kernels for 12%

profile of v4, /device:TPU:1, one launch (start us, length us, event | category | flops | bytes accessed | tf_op | source)
XLA Modules:
  0.0 29.7 jit_solution(14104790378851541868)
XLA Ops:
  0.6 0.0 copy-start.2
  0.6 0.0 copy-start.1
  0.6 7.8 %collective-permute-start.3 = (bf16[320,128]{1,0:T(8,128)(2,1)}, bf16[320,128]{1,0:T(8,128)(2,1)S(1)}, u32[]{:S(2)}, u32[]{:S(2)}) collective-permute-start(bf16[320,128]{1,0:T(8,128)(2,1)} %bitcast.6), channel_id=1, source_target_pairs={{0,128},{16,144},{32,160},{48,176},{64,192},{80,208},{96,224},{112... | collective-permute-start | bytes 245768 | tf_op jit(solution)/shard_map/ppermute | solution.py:33
  8.5 0.0 copy-start
  8.5 0.0 copy-done.2
  8.5 2.7 %collective-permute-start.2 = (bf16[320,128]{1,0:T(8,128)(2,1)S(1)}, bf16[320,128]{1,0:T(8,128)(2,1)S(1)}, u32[]{:S(2)}, u32[]{:S(2)}) collective-permute-start(bf16[320,128]{1,0:T(8,128)(2,1)S(1)} %bitcast.7), channel_id=1, source_target_pairs={{0,96},{16,112},{32,64},{48,80},{64,32},{80,48},{96,0},{112,16},{1... | collective-permute-start | bytes 245768 | tf_op jit(solution)/shard_map/ppermute | solution.py:33
  11.2 0.0 collective-permute-start.1
  11.2 1.3 %collective-permute-start = (bf16[320,128]{1,0:T(8,128)(2,1)S(1)}, bf16[320,128]{1,0:T(8,128)(2,1)S(1)}, u32[]{:S(2)}, u32[]{:S(2)}) collective-permute-start(bf16[320,128]{1,0:T(8,128)(2,1)S(1)} %bitcast.9), channel_id=1, source_target_pairs={{0,32},{16,80},{32,0},{48,112},{64,96},{80,16},{96,64},{112,48},{1... | collective-permute-start | bytes 245768 | tf_op jit(solution)/shard_map/ppermute | solution.py:33
  12.5 0.0 collective-permute-done.3.refs_4_
  12.5 2.6 %collective-permute-start.6 = (bf16[320,128]{1,0:T(8,128)(2,1)S(1)}, bf16[320,128]{1,0:T(8,128)(2,1)S(1)}, u32[]{:S(2)}, u32[]{:S(2)}) collective-permute-start(bf16[320,128]{1,0:T(8,128)(2,1)S(1)} %collective-permute-done.3.refs_4_), channel_id=1, source_target_pairs={{0,96},{16,112},{32,64},{48,80},{64,32},{80,48},{96,0},{112,16},{1... | collective-permute-start | bytes 245768 | tf_op jit(solution)/shard_map/ppermute | solution.py:33
  15.1 0.0 collective-permute-start.5
  15.1 0.0 collective-permute-done.2.refs_3_
  15.1 1.3 %collective-permute-start.4 = (bf16[320,128]{1,0:T(8,128)(2,1)S(1)}, bf16[320,128]{1,0:T(8,128)(2,1)S(1)}, u32[]{:S(2)}, u32[]{:S(2)}) collective-permute-start(bf16[320,128]{1,0:T(8,128)(2,1)S(1)} %collective-permute-done.3.refs_4_), channel_id=1, source_target_pairs={{0,32},{16,80},{32,0},{48,112},{64,96},{80,16},{96,64},{112,48},{1... | collective-permute-start | bytes 245768 | tf_op jit(solution)/shard_map/ppermute | solution.py:33
  16.4 0.0 collective-permute-done.1.refs_2_
  16.4 0.0 collective-permute-done.refs_1_
  16.4 0.0 copy-done.1
  16.4 0.0 copy-done
  16.4 2.0 %shard_map.51 = (bf16[128,5120]{1,0:T(8,128)(2,1)}, f32[2048,128]{1,0:T(8,128)S(1)}) custom-call(bf16[320,128]{1,0:T(8,128)(2,1)S(1)} %bitcast.10, bf16[320,128]{1,0:T(8,128)(2,1)S(1)} %collective-permute-done.refs_1_, bf16[320,128]{1,0:T(8,128)(2,1)S(1)} %collective-permute-done.1.refs_2_, bf16[320,128]{1,0:T(8,128)(2,1)S(1)} %collective-permute-done.2.refs_3_, ...), custom_call_target="tpu_custom_call" | custom-call | flops 1342177280 | bytes 2097152 | tf_op jit(solution)/shard_map/pallas_call | solution.py:183
  18.4 0.0 collective-permute-done.6.refs_2_.refs_7_
  18.4 0.3 collective-permute-done.5.refs_1_.refs_6_
  18.7 1.7 %collective-permute-done.4.refs_0_.refs_5_ = bf16[320,128]{1,0:T(8,128)(2,1)S(1)} collective-permute-done((bf16[320,128]{1,0:T(8,128)(2,1)S(1)}, bf16[320,128]{1,0:T(8,128)(2,1)S(1)}, u32[]{:S(2)}, u32[]{:S(2)}) %collective-permute-start.4) | collective-permute-done | bytes 81952 | tf_op jit(solution)/shard_map/ppermute | solution.py:33
  20.5 2.3 %collective-permute-start.7 = (bf16[2560,128]{1,0:T(8,128)(2,1)S(1)}, bf16[2560,128]{1,0:T(8,128)(2,1)S(1)}, u32[]{:S(2)}, u32[]{:S(2)}) collective-permute-start(bf16[2560,128]{1,0:T(8,128)(2,1)S(1)} %constant_dynamic-update-slice_fusion), channel_id=1, source_target_pairs={{0,16},{16,0},{32,48},{48,32},{64,80},{80,64},{96,112},{112,96},{1... | collective-permute-start | bytes 1966088 | tf_op jit(solution)/shard_map/ppermute | solution.py:33
  22.7 1.5 %shard_map.52 = (bf16[128,5120]{1,0:T(8,128)(2,1)}, f32[2048,128]{1,0:T(8,128)S(1)}) custom-call(bf16[320,128]{1,0:T(8,128)(2,1)S(1)} %collective-permute-done.4.refs_0_.refs_5_, bf16[320,128]{1,0:T(8,128)(2,1)S(1)} %collective-permute-done.5.refs_1_.refs_6_, ...), custom_call_target="tpu_custom_call", output_to_operand_aliasing={{0}: (6, {}), {1}: (5, {})} | custom-call | flops 805306368 | bytes 2097152 | tf_op jit(solution)/shard_map/pallas_call | solution.py:183
  24.2 0.2 collective-permute-done.7.refs_8_
  24.5 5.2 %shard_map.53 = (bf16[128,5120]{1,0:T(8,128)(2,1)}, bf16[2048,128]{1,0:T(8,128)(2,1)}) custom-call(bf16[320,128]{1,0:T(8,128)(2,1)S(1)} %bitcast.12, bf16[320,128]{1,0:T(8,128)(2,1)S(1)} %collective-permute-done.refs_1_, bf16[320,128]{1,0:T(8,128)(2,1)S(1)} %collective-permute-done.1.refs_2_, ...), custom_call_target="tpu_custom_call", output_to_operand_aliasing={{0}: (12, {})} | custom-call | flops 3221225472 | bytes 2097152 | tf_op jit(solution)/shard_map/pallas_call | solution.py:183
  (9 shorter events, 0.1 us)
Async XLA Ops:
  0.6 7.9 %copy-start.2 = (bf16[128,320]{0,1:T(8,128)(2,1)S(1)}, bf16[128,320]{0,1:T(8,128)(2,1)}, u32[]{:S(2)}) copy-start(bf16[128,320]{0,1:T(8,128)(2,1)} %param.3) | copy-start | bytes 245764
  0.6 15.7 %copy-start.1 = (bf16[1,128,5120]{2,1,0:T(8,128)(2,1)S(1)}, bf16[1,128,5120]{2,1,0:T(8,128)(2,1)}, u32[]{:S(2)}) copy-start(bf16[1,128,5120]{2,1,0:T(8,128)(2,1)} %param.4) | copy-start | bytes 3932164
  0.6 11.8 %collective-permute-start.3 = (bf16[320,128]{1,0:T(8,128)(2,1)}, bf16[320,128]{1,0:T(8,128)(2,1)S(1)}, u32[]{:S(2)}, u32[]{:S(2)}) collective-permute-start(bf16[320,128]{1,0:T(8,128)(2,1)} %bitcast.6), channel_id=1, source_target_pairs={{0,128},{16,144},{32,160},{48,176},{64,192},{80,208},{96,224},{112... | collective-permute-start | bytes 245768 | tf_op jit(solution)/shard_map/ppermute | solution.py:33
  8.5 7.9 %copy-start = (bf16[2048,5120]{1,0:T(8,128)(2,1)S(1)}, bf16[2048,5120]{1,0:T(8,128)(2,1)}, u32[]{:S(2)}) copy-start(bf16[2048,5120]{1,0:T(8,128)(2,1)} %refs_10_.1) | copy-start | bytes 62914564
  8.5 6.6 %collective-permute-start.2 = (bf16[320,128]{1,0:T(8,128)(2,1)S(1)}, bf16[320,128]{1,0:T(8,128)(2,1)S(1)}, u32[]{:S(2)}, u32[]{:S(2)}) collective-permute-start(bf16[320,128]{1,0:T(8,128)(2,1)S(1)} %bitcast.7), channel_id=1, source_target_pairs={{0,96},{16,112},{32,64},{48,80},{64,32},{80,48},{96,0},{112,16},{1... | collective-permute-start | bytes 245768 | tf_op jit(solution)/shard_map/ppermute | solution.py:33
  11.2 5.1 %collective-permute-start.1 = (bf16[320,128]{1,0:T(8,128)(2,1)S(1)}, bf16[320,128]{1,0:T(8,128)(2,1)S(1)}, u32[]{:S(2)}, u32[]{:S(2)}) collective-permute-start(bf16[320,128]{1,0:T(8,128)(2,1)S(1)} %bitcast.8), channel_id=1, source_target_pairs={{0,64},{16,48},{32,96},{48,16},{64,0},{80,112},{96,32},{112,80},{1... | collective-permute-start | bytes 245768 | tf_op jit(solution)/shard_map/ppermute | solution.py:33
  11.2 5.1 %collective-permute-start = (bf16[320,128]{1,0:T(8,128)(2,1)S(1)}, bf16[320,128]{1,0:T(8,128)(2,1)S(1)}, u32[]{:S(2)}, u32[]{:S(2)}) collective-permute-start(bf16[320,128]{1,0:T(8,128)(2,1)S(1)} %bitcast.9), channel_id=1, source_target_pairs={{0,32},{16,80},{32,0},{48,112},{64,96},{80,16},{96,64},{112,48},{1... | collective-permute-start | bytes 245768 | tf_op jit(solution)/shard_map/ppermute | solution.py:33
  12.5 5.9 %collective-permute-start.6 = (bf16[320,128]{1,0:T(8,128)(2,1)S(1)}, bf16[320,128]{1,0:T(8,128)(2,1)S(1)}, u32[]{:S(2)}, u32[]{:S(2)}) collective-permute-start(bf16[320,128]{1,0:T(8,128)(2,1)S(1)} %collective-permute-done.3.refs_4_), channel_id=1, source_target_pairs={{0,96},{16,112},{32,64},{48,80},{64,32},{80,48},{96,0},{112,16},{1... | collective-permute-start | bytes 245768 | tf_op jit(solution)/shard_map/ppermute | solution.py:33
  15.1 3.6 %collective-permute-start.5 = (bf16[320,128]{1,0:T(8,128)(2,1)S(1)}, bf16[320,128]{1,0:T(8,128)(2,1)S(1)}, u32[]{:S(2)}, u32[]{:S(2)}) collective-permute-start(bf16[320,128]{1,0:T(8,128)(2,1)S(1)} %collective-permute-done.3.refs_4_), channel_id=1, source_target_pairs={{0,64},{16,48},{32,96},{48,16},{64,0},{80,112},{96,32},{112,80},{1... | collective-permute-start | bytes 245768 | tf_op jit(solution)/shard_map/ppermute | solution.py:33
  15.1 5.3 %collective-permute-start.4 = (bf16[320,128]{1,0:T(8,128)(2,1)S(1)}, bf16[320,128]{1,0:T(8,128)(2,1)S(1)}, u32[]{:S(2)}, u32[]{:S(2)}) collective-permute-start(bf16[320,128]{1,0:T(8,128)(2,1)S(1)} %collective-permute-done.3.refs_4_), channel_id=1, source_target_pairs={{0,32},{16,80},{32,0},{48,112},{64,96},{80,16},{96,64},{112,48},{1... | collective-permute-start | bytes 245768 | tf_op jit(solution)/shard_map/ppermute | solution.py:33
  20.5 4.0 %collective-permute-start.7 = (bf16[2560,128]{1,0:T(8,128)(2,1)S(1)}, bf16[2560,128]{1,0:T(8,128)(2,1)S(1)}, u32[]{:S(2)}, u32[]{:S(2)}) collective-permute-start(bf16[2560,128]{1,0:T(8,128)(2,1)S(1)} %constant_dynamic-update-slice_fusion), channel_id=1, source_target_pairs={{0,16},{16,0},{32,48},{48,32},{64,80},{80,64},{96,112},{112,96},{1... | collective-permute-start | bytes 1966088 | tf_op jit(solution)/shard_map/ppermute | solution.py:33

commit v5 on v4

--- a/solution.py
+++ b/solution.py
@@ -10,7 +10,8 @@
 TILE = 128
 EPSILON = 1e-06
 TOKEN_BLOCK = 512
-STEPS = ((0, 0), (1, 2), (2, 1), (3, 3))
+STEPS = ((0, 0), (1, 3), (3, 1), (2, 2))
+FAR_STEPS = ((0, 0), (1, 2), (2, 1), (3, 3))
 OTHER_SLOT = (0, 2, 1, 3)
 CHIP_COLUMNS = 5 * TILE
 WHOLE = 2 * TILE
@@ -40,7 +41,7 @@
 def chip_start(slot, far, half_width):
     replica = lax.axis_index("replica")
     half, y = replica >> 3, (replica >> 1) & 3
-    step = STEPS[slot]
+    step = (FAR_STEPS if far else STEPS)[slot]
     chip = y ^ (step[0] + (replica & 1) * (step[1] - step[0]))
     side = 1 - half if far else half
     return side * half_width + chip * CHIP_COLUMNS
@@ -209,7 +210,7 @@
     own, anchor = lax.optimization_barrier((piece, anchor))
     far_piece = send(piece, dz=1)
     near = [own] + [send(own, dy=step) for step in STEPS[1:]]
-    far = [far_piece] + [send(far_piece, dy=step) for step in STEPS[1:]]
+    far = [far_piece] + [send(far_piece, dy=step) for step in FAR_STEPS[1:]]
     done = whole_part((0, 1, 2, 3, 4), near + far[:1], held, tokens, anchor)
     near, far, done = lax.optimization_barrier((near, far, done))
     others = send(jnp.concatenate(near + far), dc=1)

time: 29.8 us -> 29.5 us (0.990)
  transfers between devices with their start and end apart: 8 -> 8, of which waited for: 3 -> 4; matrix products, arithmetic and copies ran while one was open for 0% -> 0% of each run, Pallas kernels for 12% -> 12%
where the time goes in v5:
time: 29.5 us; the launch traced here: 29.4 us
  starting transfers between devices  18 us (61%)
  Pallas kernels  8.67 us (29%)
  waiting for transfers between devices  1.93 us (7%)
  between operations  0.71 us (2%)
    ppermute x8, starting transfers between devices, send(): return lax.ppermute(value, 'replica', moved(**offset))  18 us
    pallas_call x3, Pallas kernels, run_kernel(): pl.pallas_call(kernel, out_shape=(jax.ShapeDtypeStruct((row_count, tokens...  8.66 us
    ppermute x8, waiting for transfers between devices, send(): return lax.ppermute(value, 'replica', moved(**offset))  1.93 us
  transfers between devices with their start and end apart: 8, of which 4 were waited for; matrix products, arithmetic and copies ran while one was open for 0% of the time, Pallas kernels for 12%

profile of v5, /device:TPU:1, one launch (start us, length us, event | category | flops | bytes accessed | tf_op | source)
XLA Modules:
  0.0 29.4 jit_solution(2873121038232839336)
XLA Ops:
  0.6 0.0 copy-start.2
  0.6 0.0 copy-start.1
  0.6 7.8 %collective-permute-start.3 = (bf16[320,128]{1,0:T(8,128)(2,1)}, bf16[320,128]{1,0:T(8,128)(2,1)S(1)}, u32[]{:S(2)}, u32[]{:S(2)}) collective-permute-start(bf16[320,128]{1,0:T(8,128)(2,1)} %bitcast.6), channel_id=1, source_target_pairs={{0,128},{16,144},{32,160},{48,176},{64,192},{80,208},{96,224},{112... | collective-permute-start | bytes 245768 | tf_op jit(solution)/shard_map/ppermute | solution.py:34
  8.5 0.0 copy-start
  8.5 0.0 copy-done.2
  8.5 2.9 %collective-permute-start.2 = (bf16[320,128]{1,0:T(8,128)(2,1)S(1)}, bf16[320,128]{1,0:T(8,128)(2,1)S(1)}, u32[]{:S(2)}, u32[]{:S(2)}) collective-permute-start(bf16[320,128]{1,0:T(8,128)(2,1)S(1)} %bitcast.7), channel_id=1, source_target_pairs={{0,64},{16,80},{32,96},{48,112},{64,0},{80,16},{96,32},{112,48},{1... | collective-permute-start | bytes 245768 | tf_op jit(solution)/shard_map/ppermute | solution.py:34
  11.4 0.4 %collective-permute-start.1 = (bf16[320,128]{1,0:T(8,128)(2,1)S(1)}, bf16[320,128]{1,0:T(8,128)(2,1)S(1)}, u32[]{:S(2)}, u32[]{:S(2)}) collective-permute-start(bf16[320,128]{1,0:T(8,128)(2,1)S(1)} %bitcast.8), channel_id=1, source_target_pairs={{0,96},{16,48},{32,64},{48,16},{64,32},{80,112},{96,0},{112,80},{1... | collective-permute-start | bytes 245768 | tf_op jit(solution)/shard_map/ppermute | solution.py:34
  11.8 0.4 %collective-permute-start = (bf16[320,128]{1,0:T(8,128)(2,1)S(1)}, bf16[320,128]{1,0:T(8,128)(2,1)S(1)}, u32[]{:S(2)}, u32[]{:S(2)}) collective-permute-start(bf16[320,128]{1,0:T(8,128)(2,1)S(1)} %bitcast.9), channel_id=1, source_target_pairs={{0,32},{16,112},{32,0},{48,80},{64,96},{80,48},{96,64},{112,16},{1... | collective-permute-start | bytes 245768 | tf_op jit(solution)/shard_map/ppermute | solution.py:34
  12.2 0.0 collective-permute-done.3.refs_4_
  12.2 2.3 %collective-permute-start.6 = (bf16[320,128]{1,0:T(8,128)(2,1)S(1)}, bf16[320,128]{1,0:T(8,128)(2,1)S(1)}, u32[]{:S(2)}, u32[]{:S(2)}) collective-permute-start(bf16[320,128]{1,0:T(8,128)(2,1)S(1)} %collective-permute-done.3.refs_4_), channel_id=1, source_target_pairs={{0,96},{16,112},{32,64},{48,80},{64,32},{80,48},{96,0},{112,16},{1... | collective-permute-start | bytes 245768 | tf_op jit(solution)/shard_map/ppermute | solution.py:34
  14.5 0.0 collective-permute-start.5
  14.5 0.0 collective-permute-done.2.refs_3_
  14.5 1.8 %collective-permute-start.4 = (bf16[320,128]{1,0:T(8,128)(2,1)S(1)}, bf16[320,128]{1,0:T(8,128)(2,1)S(1)}, u32[]{:S(2)}, u32[]{:S(2)}) collective-permute-start(bf16[320,128]{1,0:T(8,128)(2,1)S(1)} %collective-permute-done.3.refs_4_), channel_id=1, source_target_pairs={{0,32},{16,80},{32,0},{48,112},{64,96},{80,16},{96,64},{112,48},{1... | collective-permute-start | bytes 245768 | tf_op jit(solution)/shard_map/ppermute | solution.py:34
  16.2 0.0 collective-permute-done.1.refs_2_
  16.2 0.1 collective-permute-done.refs_1_
  16.3 0.0 copy-done.1
  16.3 0.0 copy-done
  16.3 2.0 %shard_map.51 = (bf16[128,5120]{1,0:T(8,128)(2,1)}, f32[2048,128]{1,0:T(8,128)S(1)}) custom-call(bf16[320,128]{1,0:T(8,128)(2,1)S(1)} %bitcast.10, bf16[320,128]{1,0:T(8,128)(2,1)S(1)} %collective-permute-done.refs_1_, bf16[320,128]{1,0:T(8,128)(2,1)S(1)} %collective-permute-done.1.refs_2_, bf16[320,128]{1,0:T(8,128)(2,1)S(1)} %collective-permute-done.2.refs_3_, ...), custom_call_target="tpu_custom_call" | custom-call | flops 1342177280 | bytes 2097152 | tf_op jit(solution)/shard_map/pallas_call | solution.py:184
  18.3 0.0 collective-permute-done.6.refs_2_.refs_7_
  18.3 0.3 collective-permute-done.5.refs_1_.refs_6_
  18.6 1.3 %collective-permute-done.4.refs_0_.refs_5_ = bf16[320,128]{1,0:T(8,128)(2,1)S(1)} collective-permute-done((bf16[320,128]{1,0:T(8,128)(2,1)S(1)}, bf16[320,128]{1,0:T(8,128)(2,1)S(1)}, u32[]{:S(2)}, u32[]{:S(2)}) %collective-permute-start.4) | collective-permute-done | bytes 81952 | tf_op jit(solution)/shard_map/ppermute | solution.py:34
  20.1 2.4 %collective-permute-start.7 = (bf16[2560,128]{1,0:T(8,128)(2,1)S(1)}, bf16[2560,128]{1,0:T(8,128)(2,1)S(1)}, u32[]{:S(2)}, u32[]{:S(2)}) collective-permute-start(bf16[2560,128]{1,0:T(8,128)(2,1)S(1)} %constant_dynamic-update-slice_fusion), channel_id=1, source_target_pairs={{0,16},{16,0},{32,48},{48,32},{64,80},{80,64},{96,112},{112,96},{1... | collective-permute-start | bytes 1966088 | tf_op jit(solution)/shard_map/ppermute | solution.py:34
  22.5 1.5 %shard_map.52 = (bf16[128,5120]{1,0:T(8,128)(2,1)}, f32[2048,128]{1,0:T(8,128)S(1)}) custom-call(bf16[320,128]{1,0:T(8,128)(2,1)S(1)} %collective-permute-done.4.refs_0_.refs_5_, bf16[320,128]{1,0:T(8,128)(2,1)S(1)} %collective-permute-done.5.refs_1_.refs_6_, ...), custom_call_target="tpu_custom_call", output_to_operand_aliasing={{0}: (6, {}), {1}: (5, {})} | custom-call | flops 805306368 | bytes 2097152 | tf_op jit(solution)/shard_map/pallas_call | solution.py:184
  23.9 0.2 collective-permute-done.7.refs_8_
  24.2 5.2 %shard_map.53 = (bf16[128,5120]{1,0:T(8,128)(2,1)}, bf16[2048,128]{1,0:T(8,128)(2,1)}) custom-call(bf16[320,128]{1,0:T(8,128)(2,1)S(1)} %bitcast.12, bf16[320,128]{1,0:T(8,128)(2,1)S(1)} %collective-permute-done.refs_1_, bf16[320,128]{1,0:T(8,128)(2,1)S(1)} %collective-permute-done.1.refs_2_, ...), custom_call_target="tpu_custom_call", output_to_operand_aliasing={{0}: (12, {})} | custom-call | flops 3221225472 | bytes 2097152 | tf_op jit(solution)/shard_map/pallas_call | solution.py:184
  (9 shorter events, 0.1 us)
Async XLA Ops:
  0.6 7.9 %copy-start.2 = (bf16[128,320]{0,1:T(8,128)(2,1)S(1)}, bf16[128,320]{0,1:T(8,128)(2,1)}, u32[]{:S(2)}) copy-start(bf16[128,320]{0,1:T(8,128)(2,1)} %param.3) | copy-start | bytes 245764
  0.6 15.7 %copy-start.1 = (bf16[1,128,5120]{2,1,0:T(8,128)(2,1)S(1)}, bf16[1,128,5120]{2,1,0:T(8,128)(2,1)}, u32[]{:S(2)}) copy-start(bf16[1,128,5120]{2,1,0:T(8,128)(2,1)} %param.4) | copy-start | bytes 3932164
  0.6 11.5 %collective-permute-start.3 = (bf16[320,128]{1,0:T(8,128)(2,1)}, bf16[320,128]{1,0:T(8,128)(2,1)S(1)}, u32[]{:S(2)}, u32[]{:S(2)}) collective-permute-start(bf16[320,128]{1,0:T(8,128)(2,1)} %bitcast.6), channel_id=1, source_target_pairs={{0,128},{16,144},{32,160},{48,176},{64,192},{80,208},{96,224},{112... | collective-permute-start | bytes 245768 | tf_op jit(solution)/shard_map/ppermute | solution.py:34
  8.5 7.8 %copy-start = (bf16[2048,5120]{1,0:T(8,128)(2,1)S(1)}, bf16[2048,5120]{1,0:T(8,128)(2,1)}, u32[]{:S(2)}) copy-start(bf16[2048,5120]{1,0:T(8,128)(2,1)} %refs_10_.1) | copy-start | bytes 62914564
  8.5 6.0 %collective-permute-start.2 = (bf16[320,128]{1,0:T(8,128)(2,1)S(1)}, bf16[320,128]{1,0:T(8,128)(2,1)S(1)}, u32[]{:S(2)}, u32[]{:S(2)}) collective-permute-start(bf16[320,128]{1,0:T(8,128)(2,1)S(1)} %bitcast.7), channel_id=1, source_target_pairs={{0,64},{16,80},{32,96},{48,112},{64,0},{80,16},{96,32},{112,48},{1... | collective-permute-start | bytes 245768 | tf_op jit(solution)/shard_map/ppermute | solution.py:34
  11.4 4.8 %collective-permute-start.1 = (bf16[320,128]{1,0:T(8,128)(2,1)S(1)}, bf16[320,128]{1,0:T(8,128)(2,1)S(1)}, u32[]{:S(2)}, u32[]{:S(2)}) collective-permute-start(bf16[320,128]{1,0:T(8,128)(2,1)S(1)} %bitcast.8), channel_id=1, source_target_pairs={{0,96},{16,48},{32,64},{48,16},{64,32},{80,112},{96,0},{112,80},{1... | collective-permute-start | bytes 245768 | tf_op jit(solution)/shard_map/ppermute | solution.py:34
  11.8 4.5 %collective-permute-start = (bf16[320,128]{1,0:T(8,128)(2,1)S(1)}, bf16[320,128]{1,0:T(8,128)(2,1)S(1)}, u32[]{:S(2)}, u32[]{:S(2)}) collective-permute-start(bf16[320,128]{1,0:T(8,128)(2,1)S(1)} %bitcast.9), channel_id=1, source_target_pairs={{0,32},{16,112},{32,0},{48,80},{64,96},{80,48},{96,64},{112,16},{1... | collective-permute-start | bytes 245768 | tf_op jit(solution)/shard_map/ppermute | solution.py:34
  12.2 6.1 %collective-permute-start.6 = (bf16[320,128]{1,0:T(8,128)(2,1)S(1)}, bf16[320,128]{1,0:T(8,128)(2,1)S(1)}, u32[]{:S(2)}, u32[]{:S(2)}) collective-permute-start(bf16[320,128]{1,0:T(8,128)(2,1)S(1)} %collective-permute-done.3.refs_4_), channel_id=1, source_target_pairs={{0,96},{16,112},{32,64},{48,80},{64,32},{80,48},{96,0},{112,16},{1... | collective-permute-start | bytes 245768 | tf_op jit(solution)/shard_map/ppermute | solution.py:34
  14.5 4.1 %collective-permute-start.5 = (bf16[320,128]{1,0:T(8,128)(2,1)S(1)}, bf16[320,128]{1,0:T(8,128)(2,1)S(1)}, u32[]{:S(2)}, u32[]{:S(2)}) collective-permute-start(bf16[320,128]{1,0:T(8,128)(2,1)S(1)} %collective-permute-done.3.refs_4_), channel_id=1, source_target_pairs={{0,64},{16,48},{32,96},{48,16},{64,0},{80,112},{96,32},{112,80},{1... | collective-permute-start | bytes 245768 | tf_op jit(solution)/shard_map/ppermute | solution.py:34
  14.5 5.5 %collective-permute-start.4 = (bf16[320,128]{1,0:T(8,128)(2,1)S(1)}, bf16[320,128]{1,0:T(8,128)(2,1)S(1)}, u32[]{:S(2)}, u32[]{:S(2)}) collective-permute-start(bf16[320,128]{1,0:T(8,128)(2,1)S(1)} %collective-permute-done.3.refs_4_), channel_id=1, source_target_pairs={{0,32},{16,80},{32,0},{48,112},{64,96},{80,16},{96,64},{112,48},{1... | collective-permute-start | bytes 245768 | tf_op jit(solution)/shard_map/ppermute | solution.py:34
  20.1 4.1 %collective-permute-start.7 = (bf16[2560,128]{1,0:T(8,128)(2,1)S(1)}, bf16[2560,128]{1,0:T(8,128)(2,1)S(1)}, u32[]{:S(2)}, u32[]{:S(2)}) collective-permute-start(bf16[2560,128]{1,0:T(8,128)(2,1)S(1)} %constant_dynamic-update-slice_fusion), channel_id=1, source_target_pairs={{0,16},{16,0},{32,48},{48,32},{64,80},{80,64},{96,112},{112,96},{1... | collective-permute-start | bytes 1966088 | tf_op jit(solution)/shard_map/ppermute | solution.py:34

commit v6 on v5

--- a/solution.py
+++ b/solution.py
@@ -11,7 +11,7 @@
 EPSILON = 1e-06
 TOKEN_BLOCK = 512
 STEPS = ((0, 0), (1, 3), (3, 1), (2, 2))
-FAR_STEPS = ((0, 0), (1, 2), (2, 1), (3, 3))
+FAR_STEPS = ((0, 0), (3, 2), (2, 3), (1, 1))
 OTHER_SLOT = (0, 2, 1, 3)
 CHIP_COLUMNS = 5 * TILE
 WHOLE = 2 * TILE

time: 29.5 us -> 30.5 us (1.034)
  waiting for transfers between devices: 1.93 us -> 2.56 us
    ppermute x8, waiting for transfers between devices: 1.93 us -> 2.56 us  [send(): return lax.ppermute(value, 'replica', moved(**offset))]
    ppermute x8, starting transfers between devices: 18 us -> 18.3 us  [send(): return lax.ppermute(value, 'replica', moved(**offset))]
  transfers between devices with their start and end apart: 8 -> 8, of which waited for: 4 -> 4; matrix products, arithmetic and copies ran while one was open for 0% -> 0% of each run, Pallas kernels for 12% -> 11%
where the time goes in v6:
time: 30.5 us; the launch traced here: 30.4 us
  starting transfers between devices  18.3 us (60%)
  Pallas kernels  8.66 us (28%)
  waiting for transfers between devices  2.56 us (8%)
  between operations  0.71 us (2%)
    ppermute x8, starting transfers between devices, send(): return lax.ppermute(value, 'replica', moved(**offset))  18.3 us
    pallas_call x3, Pallas kernels, run_kernel(): pl.pallas_call(kernel, out_shape=(jax.ShapeDtypeStruct((row_count, tokens...  8.66 us
    ppermute x8, waiting for transfers between devices, send(): return lax.ppermute(value, 'replica', moved(**offset))  2.56 us
  transfers between devices with their start and end apart: 8, of which 4 were waited for; matrix products, arithmetic and copies ran while one was open for 0% of the time, Pallas kernels for 11%

profile of v6, /device:TPU:1, one launch (start us, length us, event | category | flops | bytes accessed | tf_op | source)
XLA Modules:
  0.0 30.4 jit_solution(15655004279010777140)
XLA Ops:
  0.6 0.0 copy-start.2
  0.6 0.0 copy-start.1
  0.6 7.8 %collective-permute-start.3 = (bf16[320,128]{1,0:T(8,128)(2,1)}, bf16[320,128]{1,0:T(8,128)(2,1)S(1)}, u32[]{:S(2)}, u32[]{:S(2)}) collective-permute-start(bf16[320,128]{1,0:T(8,128)(2,1)} %bitcast.6), channel_id=1, source_target_pairs={{0,128},{16,144},{32,160},{48,176},{64,192},{80,208},{96,224},{112... | collective-permute-start | bytes 245768 | tf_op jit(solution)/shard_map/ppermute | solution.py:34
  8.5 0.0 copy-start
  8.5 0.0 copy-done.2
  8.5 2.9 %collective-permute-start.2 = (bf16[320,128]{1,0:T(8,128)(2,1)S(1)}, bf16[320,128]{1,0:T(8,128)(2,1)S(1)}, u32[]{:S(2)}, u32[]{:S(2)}) collective-permute-start(bf16[320,128]{1,0:T(8,128)(2,1)S(1)} %bitcast.7), channel_id=1, source_target_pairs={{0,64},{16,80},{32,96},{48,112},{64,0},{80,16},{96,32},{112,48},{1... | collective-permute-start | bytes 245768 | tf_op jit(solution)/shard_map/ppermute | solution.py:34
  11.4 0.4 %collective-permute-start.1 = (bf16[320,128]{1,0:T(8,128)(2,1)S(1)}, bf16[320,128]{1,0:T(8,128)(2,1)S(1)}, u32[]{:S(2)}, u32[]{:S(2)}) collective-permute-start(bf16[320,128]{1,0:T(8,128)(2,1)S(1)} %bitcast.8), channel_id=1, source_target_pairs={{0,96},{16,48},{32,64},{48,16},{64,32},{80,112},{96,0},{112,80},{1... | collective-permute-start | bytes 245768 | tf_op jit(solution)/shard_map/ppermute | solution.py:34
  11.8 0.4 %collective-permute-start = (bf16[320,128]{1,0:T(8,128)(2,1)S(1)}, bf16[320,128]{1,0:T(8,128)(2,1)S(1)}, u32[]{:S(2)}, u32[]{:S(2)}) collective-permute-start(bf16[320,128]{1,0:T(8,128)(2,1)S(1)} %bitcast.9), channel_id=1, source_target_pairs={{0,32},{16,112},{32,0},{48,80},{64,96},{80,48},{96,64},{112,16},{1... | collective-permute-start | bytes 245768 | tf_op jit(solution)/shard_map/ppermute | solution.py:34
  12.2 0.0 collective-permute-done.3.refs_4_
  12.2 0.9 %collective-permute-start.6 = (bf16[320,128]{1,0:T(8,128)(2,1)S(1)}, bf16[320,128]{1,0:T(8,128)(2,1)S(1)}, u32[]{:S(2)}, u32[]{:S(2)}) collective-permute-start(bf16[320,128]{1,0:T(8,128)(2,1)S(1)} %collective-permute-done.3.refs_4_), channel_id=1, source_target_pairs={{0,32},{16,48},{32,0},{48,16},{64,96},{80,112},{96,64},{112,80},{1... | collective-permute-start | bytes 245768 | tf_op jit(solution)/shard_map/ppermute | solution.py:34
  13.0 1.9 %collective-permute-start.5 = (bf16[320,128]{1,0:T(8,128)(2,1)S(1)}, bf16[320,128]{1,0:T(8,128)(2,1)S(1)}, u32[]{:S(2)}, u32[]{:S(2)}) collective-permute-start(bf16[320,128]{1,0:T(8,128)(2,1)S(1)} %collective-permute-done.3.refs_4_), channel_id=1, source_target_pairs={{0,64},{16,112},{32,96},{48,80},{64,0},{80,48},{96,32},{112,16},{1... | collective-permute-start | bytes 245768 | tf_op jit(solution)/shard_map/ppermute | solution.py:34
  14.9 0.0 collective-permute-done.2.refs_3_
  14.9 1.3 %collective-permute-start.4 = (bf16[320,128]{1,0:T(8,128)(2,1)S(1)}, bf16[320,128]{1,0:T(8,128)(2,1)S(1)}, u32[]{:S(2)}, u32[]{:S(2)}) collective-permute-start(bf16[320,128]{1,0:T(8,128)(2,1)S(1)} %collective-permute-done.3.refs_4_), channel_id=1, source_target_pairs={{0,96},{16,80},{32,64},{48,112},{64,32},{80,16},{96,0},{112,48},{1... | collective-permute-start | bytes 245768 | tf_op jit(solution)/shard_map/ppermute | solution.py:34
  16.2 0.0 collective-permute-done.1.refs_2_
  16.2 0.1 collective-permute-done.refs_1_
  16.3 0.0 copy-done.1
  16.3 0.0 copy-done
  16.3 2.0 %shard_map.51 = (bf16[128,5120]{1,0:T(8,128)(2,1)}, f32[2048,128]{1,0:T(8,128)S(1)}) custom-call(bf16[320,128]{1,0:T(8,128)(2,1)S(1)} %bitcast.10, bf16[320,128]{1,0:T(8,128)(2,1)S(1)} %collective-permute-done.refs_1_, bf16[320,128]{1,0:T(8,128)(2,1)S(1)} %collective-permute-done.1.refs_2_, bf16[320,128]{1,0:T(8,128)(2,1)S(1)} %collective-permute-done.2.refs_3_, ...), custom_call_target="tpu_custom_call" | custom-call | flops 1342177280 | bytes 2097152 | tf_op jit(solution)/shard_map/pallas_call | solution.py:184
  18.3 0.0 collective-permute-done.6.refs_2_.refs_7_
  18.3 0.3 %collective-permute-done.5.refs_1_.refs_6_ = bf16[320,128]{1,0:T(8,128)(2,1)S(1)} collective-permute-done((bf16[320,128]{1,0:T(8,128)(2,1)S(1)}, bf16[320,128]{1,0:T(8,128)(2,1)S(1)}, u32[]{:S(2)}, u32[]{:S(2)}) %collective-permute-start.5) | collective-permute-done | bytes 81952 | tf_op jit(solution)/shard_map/ppermute | solution.py:34
  18.7 1.9 %collective-permute-done.4.refs_0_.refs_5_ = bf16[320,128]{1,0:T(8,128)(2,1)S(1)} collective-permute-done((bf16[320,128]{1,0:T(8,128)(2,1)S(1)}, bf16[320,128]{1,0:T(8,128)(2,1)S(1)}, u32[]{:S(2)}, u32[]{:S(2)}) %collective-permute-start.4) | collective-permute-done | bytes 81952 | tf_op jit(solution)/shard_map/ppermute | solution.py:34
  20.7 2.8 %collective-permute-start.7 = (bf16[2560,128]{1,0:T(8,128)(2,1)S(1)}, bf16[2560,128]{1,0:T(8,128)(2,1)S(1)}, u32[]{:S(2)}, u32[]{:S(2)}) collective-permute-start(bf16[2560,128]{1,0:T(8,128)(2,1)S(1)} %constant_dynamic-update-slice_fusion), channel_id=1, source_target_pairs={{0,16},{16,0},{32,48},{48,32},{64,80},{80,64},{96,112},{112,96},{1... | collective-permute-start | bytes 1966088 | tf_op jit(solution)/shard_map/ppermute | solution.py:34
  23.5 1.5 %shard_map.52 = (bf16[128,5120]{1,0:T(8,128)(2,1)}, f32[2048,128]{1,0:T(8,128)S(1)}) custom-call(bf16[320,128]{1,0:T(8,128)(2,1)S(1)} %collective-permute-done.4.refs_0_.refs_5_, bf16[320,128]{1,0:T(8,128)(2,1)S(1)} %collective-permute-done.5.refs_1_.refs_6_, ...), custom_call_target="tpu_custom_call", output_to_operand_aliasing={{0}: (6, {}), {1}: (5, {})} | custom-call | flops 805306368 | bytes 2097152 | tf_op jit(solution)/shard_map/pallas_call | solution.py:184
  25.0 0.2 collective-permute-done.7.refs_8_
  25.2 5.2 %shard_map.53 = (bf16[128,5120]{1,0:T(8,128)(2,1)}, bf16[2048,128]{1,0:T(8,128)(2,1)}) custom-call(bf16[320,128]{1,0:T(8,128)(2,1)S(1)} %bitcast.12, bf16[320,128]{1,0:T(8,128)(2,1)S(1)} %collective-permute-done.refs_1_, bf16[320,128]{1,0:T(8,128)(2,1)S(1)} %collective-permute-done.1.refs_2_, ...), custom_call_target="tpu_custom_call", output_to_operand_aliasing={{0}: (12, {})} | custom-call | flops 3221225472 | bytes 2097152 | tf_op jit(solution)/shard_map/pallas_call | solution.py:184
  (9 shorter events, 0.1 us)
Async XLA Ops:
  0.6 7.9 %copy-start.2 = (bf16[128,320]{0,1:T(8,128)(2,1)S(1)}, bf16[128,320]{0,1:T(8,128)(2,1)}, u32[]{:S(2)}) copy-start(bf16[128,320]{0,1:T(8,128)(2,1)} %param.3) | copy-start | bytes 245764
  0.6 15.7 %copy-start.1 = (bf16[1,128,5120]{2,1,0:T(8,128)(2,1)S(1)}, bf16[1,128,5120]{2,1,0:T(8,128)(2,1)}, u32[]{:S(2)}) copy-start(bf16[1,128,5120]{2,1,0:T(8,128)(2,1)} %param.4) | copy-start | bytes 3932164
  0.6 11.5 %collective-permute-start.3 = (bf16[320,128]{1,0:T(8,128)(2,1)}, bf16[320,128]{1,0:T(8,128)(2,1)S(1)}, u32[]{:S(2)}, u32[]{:S(2)}) collective-permute-start(bf16[320,128]{1,0:T(8,128)(2,1)} %bitcast.6), channel_id=1, source_target_pairs={{0,128},{16,144},{32,160},{48,176},{64,192},{80,208},{96,224},{112... | collective-permute-start | bytes 245768 | tf_op jit(solution)/shard_map/ppermute | solution.py:34
  8.5 7.8 %copy-start = (bf16[2048,5120]{1,0:T(8,128)(2,1)S(1)}, bf16[2048,5120]{1,0:T(8,128)(2,1)}, u32[]{:S(2)}) copy-start(bf16[2048,5120]{1,0:T(8,128)(2,1)} %refs_10_.1) | copy-start | bytes 62914564
  8.5 6.5 %collective-permute-start.2 = (bf16[320,128]{1,0:T(8,128)(2,1)S(1)}, bf16[320,128]{1,0:T(8,128)(2,1)S(1)}, u32[]{:S(2)}, u32[]{:S(2)}) collective-permute-start(bf16[320,128]{1,0:T(8,128)(2,1)S(1)} %bitcast.7), channel_id=1, source_target_pairs={{0,64},{16,80},{32,96},{48,112},{64,0},{80,16},{96,32},{112,48},{1... | collective-permute-start | bytes 245768 | tf_op jit(solution)/shard_map/ppermute | solution.py:34
  11.4 4.8 %collective-permute-start.1 = (bf16[320,128]{1,0:T(8,128)(2,1)S(1)}, bf16[320,128]{1,0:T(8,128)(2,1)S(1)}, u32[]{:S(2)}, u32[]{:S(2)}) collective-permute-start(bf16[320,128]{1,0:T(8,128)(2,1)S(1)} %bitcast.8), channel_id=1, source_target_pairs={{0,96},{16,48},{32,64},{48,16},{64,32},{80,112},{96,0},{112,80},{1... | collective-permute-start | bytes 245768 | tf_op jit(solution)/shard_map/ppermute | solution.py:34
  11.8 4.5 %collective-permute-start = (bf16[320,128]{1,0:T(8,128)(2,1)S(1)}, bf16[320,128]{1,0:T(8,128)(2,1)S(1)}, u32[]{:S(2)}, u32[]{:S(2)}) collective-permute-start(bf16[320,128]{1,0:T(8,128)(2,1)S(1)} %bitcast.9), channel_id=1, source_target_pairs={{0,32},{16,112},{32,0},{48,80},{64,96},{80,48},{96,64},{112,16},{1... | collective-permute-start | bytes 245768 | tf_op jit(solution)/shard_map/ppermute | solution.py:34
  12.2 6.1 %collective-permute-start.6 = (bf16[320,128]{1,0:T(8,128)(2,1)S(1)}, bf16[320,128]{1,0:T(8,128)(2,1)S(1)}, u32[]{:S(2)}, u32[]{:S(2)}) collective-permute-start(bf16[320,128]{1,0:T(8,128)(2,1)S(1)} %collective-permute-done.3.refs_4_), channel_id=1, source_target_pairs={{0,32},{16,48},{32,0},{48,16},{64,96},{80,112},{96,64},{112,80},{1... | collective-permute-start | bytes 245768 | tf_op jit(solution)/shard_map/ppermute | solution.py:34
  13.0 5.6 %collective-permute-start.5 = (bf16[320,128]{1,0:T(8,128)(2,1)S(1)}, bf16[320,128]{1,0:T(8,128)(2,1)S(1)}, u32[]{:S(2)}, u32[]{:S(2)}) collective-permute-start(bf16[320,128]{1,0:T(8,128)(2,1)S(1)} %collective-permute-done.3.refs_4_), channel_id=1, source_target_pairs={{0,64},{16,112},{32,96},{48,80},{64,0},{80,48},{96,32},{112,16},{1... | collective-permute-start | bytes 245768 | tf_op jit(solution)/shard_map/ppermute | solution.py:34
  14.9 5.6 %collective-permute-start.4 = (bf16[320,128]{1,0:T(8,128)(2,1)S(1)}, bf16[320,128]{1,0:T(8,128)(2,1)S(1)}, u32[]{:S(2)}, u32[]{:S(2)}) collective-permute-start(bf16[320,128]{1,0:T(8,128)(2,1)S(1)} %collective-permute-done.3.refs_4_), channel_id=1, source_target_pairs={{0,96},{16,80},{32,64},{48,112},{64,32},{80,16},{96,0},{112,48},{1... | collective-permute-start | bytes 245768 | tf_op jit(solution)/shard_map/ppermute | solution.py:34
  20.7 4.5 %collective-permute-start.7 = (bf16[2560,128]{1,0:T(8,128)(2,1)S(1)}, bf16[2560,128]{1,0:T(8,128)(2,1)S(1)}, u32[]{:S(2)}, u32[]{:S(2)}) collective-permute-start(bf16[2560,128]{1,0:T(8,128)(2,1)S(1)} %constant_dynamic-update-slice_fusion), channel_id=1, source_target_pairs={{0,16},{16,0},{32,48},{48,32},{64,80},{80,64},{96,112},{112,96},{1... | collective-permute-start | bytes 1966088 | tf_op jit(solution)/shard_map/ppermute | solution.py:34
